TPU v7x, 128 devices: a whole 4x4x4 slice. The times are simulated.
128 devices in a mesh: row: 16 (over x, z), col: 8 (over y, core).
Axes of the slice: x: 4, y: 4, z: 4, core: 2. Of those that a mesh axis runs over, the one named last changes fastest.
Arguments:
- front: bfloat16 [16384, 16384], P('row', 'col'), may hold values from -6 to 6
- tiles: bfloat16 [16384, 128, 128], P(('row', 'col')), may hold values from -6 to 6
- counts: int32 [128], P(('row', 'col')), may hold values from 64 to 128, as said below
- dest_owner: int32 [16384, 1], P(('row', 'col')), may hold values from 0 to 127; in each aligned block of 128 rows (0 to 127, 128 to 255, ...) at most 2 rows name the same one
- dest_slot: int32 [16384], P(('row', 'col')), may hold values from 0 to 127
- omega: bfloat16 [512, 128], replicated, may hold values from -0.25 to 0.25
- psi: bfloat16 [512, 128], replicated, may hold values from -0.25 to 0.25
- core: bfloat16 [128, 128], replicated, may hold values from -0.00390625 to 0.00390625
Outputs:
- updated: bfloat16 [16384, 16384], P('row', 'col')
Inputs may be any that keep to these rules, and one draw needn't show every extreme that they name: `counts`: some device has all 128 tiles live in every draw. `dest_owner`: among the 128 tiles of one device at most 2 name the same owner, live or not; this is reached.
All inputs are finite; a program needn't handle non-finite values.
Results may differ from a plain program's by a relative error of at most 0.0085.
Values may be sent and summed in bfloat16 or wider, within the bound.
A program may use at most 128 MiB of HBM per device.

v0:
```python
import jax
import jax.numpy as jnp
from jax import lax
from jax.sharding import PartitionSpec as P

PB = 512
TILE = 128
PANELS = 10
CAP = 2


def broadcast(block, axis, owner):
    block = jnp.where(lax.axis_index(axis) == owner, block, jnp.zeros_like(block))
    return lax.psum(block, axis)


def shards(front, tiles, counts, dest_owner, dest_slot, omega, psi, core):
    n_row = lax.axis_size("row")
    n_col = lax.axis_size("col")
    n_dev = n_row * n_col
    row_width = front.shape[0]
    col_width = front.shape[1]
    row_tiles = row_width // TILE
    col_tiles = col_width // TILE
    strips = tiles.shape[0]
    owners = dest_owner[:, 0]
    strip_ids = jnp.arange(strips, dtype=jnp.int32)
    same = owners[:, None] == owners[None, :]
    before = strip_ids[None, :] < strip_ids[:, None]
    ranks = jnp.sum((same & before).astype(jnp.int32), axis=1)
    target = owners * CAP + ranks
    valid = strip_ids < counts[0]
    live = jnp.where(valid[:, None, None], tiles, jnp.zeros_like(tiles))
    send_tiles = jnp.zeros((n_dev * CAP, TILE, TILE), jnp.bfloat16).at[target].set(live)
    send_slots = jnp.zeros((n_dev * CAP,), jnp.int32).at[target].set(dest_slot)
    got_tiles, got_slots = (
        lax.all_to_all(send_tiles, ("row", "col"), split_axis=0, concat_axis=0, tiled=True),
        lax.all_to_all(send_slots, ("row", "col"), split_axis=0, concat_axis=0, tiled=True),
    )
    got_tiles = got_tiles.reshape(n_dev * CAP, TILE * TILE)
    onehot = (
        got_slots[:, None] == jnp.arange(row_tiles * col_tiles, dtype=jnp.int32)[None, :]
    ).astype(jnp.bfloat16)
    summed = lax.dot_general(
        onehot, got_tiles, (((0,), (0,)), ((), ())), preferred_element_type=jnp.float32
    )
    summed = (
        summed.reshape(row_tiles, col_tiles, TILE, TILE)
        .transpose(0, 2, 1, 3)
        .reshape(row_width, col_width)
    )
    grid = front.astype(jnp.float32) + summed
    row_pos = lax.axis_index("row") * row_width + jnp.arange(row_width, dtype=jnp.int32)
    col_pos = lax.axis_index("col") * col_width + jnp.arange(col_width, dtype=jnp.int32)

    def panel_step(panel, grid):
        lower = panel * PB
        upper = lower + PB
        row_root = lower // row_width
        col_root = lower // col_width
        own_cols = lax.dynamic_slice_in_dim(grid, lower % col_width, PB, 1).astype(jnp.bfloat16)
        own_rows = lax.dynamic_slice_in_dim(grid, lower % row_width, PB, 0).astype(jnp.bfloat16)
        pcols = broadcast(own_cols, "col", col_root)
        prows = broadcast(own_rows, "row", row_root)
        basis = jnp.dot(pcols, omega, preferred_element_type=jnp.float32).astype(jnp.bfloat16)
        left = jnp.dot(basis, core, preferred_element_type=jnp.float32).astype(jnp.bfloat16)
        right = lax.dot_general(
            psi, prows, (((0,), (0,)), ((), ())), preferred_element_type=jnp.float32
        ).astype(jnp.bfloat16)
        keep_rows = (row_pos >= upper).astype(jnp.float32)
        keep_cols = (col_pos >= upper).astype(jnp.float32)
        product = jnp.dot(left, right, preferred_element_type=jnp.float32)
        return grid - product * keep_rows[:, None] * keep_cols[None, :]

    grid = lax.fori_loop(0, PANELS, panel_step, grid)
    return grid.astype(jnp.bfloat16)


def solution(mesh):
    in_specs = (
        P("row", "col"),
        P(("row", "col"), None, None),
        P(("row", "col")),
        P(("row", "col"), None),
        P(("row", "col")),
        P(),
        P(),
        P(),
    )
    out_specs = P("row", "col")
    return jax.shard_map(shards, mesh=mesh, in_specs=in_specs, out_specs=out_specs, check_vma=False)
```

profile of v0, /device:TPU:80, one launch (start us, length us, event | category | flops | bytes accessed | tf_op | source)
XLA Modules:
  0.0 1870.8 jit_solution(11654374615386654765)
XLA Ops:
  10.0 9.9 all-to-all-start
  20.6 4.6 broadcast_select_fusion
  25.2 5.3 broadcast_in_dim.31
  30.5 19.3 %scatter_fusion = bf16[256,128,128]{2,1,0:T(8,128)(2,1)} fusion(bf16[256,128,128]{2,1,0:T(8,128)(2,1)} %broadcast_in_dim.31, s32[128]{0:T(128)S(1)} %fusion.15, bf16[128,128,128]{2,1,0:T(8,128)(2,1)} %broadcast_select_fusion), kind=kCustom, calls=%fused_computation.1 | custom fusion | bytes 12583424 | tf_op jit(solution)/shard_map/scatter | solution.py:34
  49.8 10.2 all-to-all-start.1
  61.5 98.4 %all-to-all-done.1 = bf16[256,128,128]{2,1,0:T(8,128)(2,1)} async-done(((bf16[256,128,128]{2,1,0:T(8,128)(2,1)}), bf16[256,128,128]{2,1,0:T(8,128)(2,1)}, u32[]{:S(2)}, u32[]{:S(2)}) %all-to-all-start.1) | async-done | bytes 8388640 | tf_op jit(solution)/shard_map/all_to_all | solution.py:37
  159.9 12.6 copy.15
  172.5 6.4 fusion.8
  178.9 7.7 bitcast_add_fusion
  186.7 1671.2 %while.17 = (s32[]{:T(128)}, f32[1024,2048]{1,0:T(8,128)}, bf16[512,128]{1,0:T(8,128)(2,1)S(1)}, bf16[128,128]{1,0:T(8,128)(2,1)S(1)}, bf16[512,128]{1,0:T(8,128...) while((s32[]{:T(128)}, f32[1024,2048]{1,0:T(8,128)}, ...), condition=%wide.region_6.7_spmd.clone, body=%wide.region_3.6_spmd.clone.sunk | while | flops 983049216 | bytes 45933320 | solution.py:75
  189.7 4.0 fusion.43
  193.8 60.4 %all-reduce.3.cloned.1.call-done = bf16[1024,512]{1,0:T(8,128)(2,1)} async-done(((bf16[1024,512]{1,0:T(8,128)(2,1)}), bf16[1024,512]{1,0:T(8,128)(2,1)}) %all-reduce.3.cloned.1.call-update) | async-done | bytes 1048592 | tf_op jit(solution)/shard_map/while/body/eval_jaxpr/psum | solution.py:14
  256.0 93.5 %all-reduce.5.cloned.1.call-done = bf16[512,2048]{1,0:T(8,128)(2,1)} async-done(((bf16[512,2048]{1,0:T(8,128)(2,1)}), bf16[512,2048]{1,0:T(8,128)(2,1)}) %all-reduce.5.cloned.1.call-update) | async-done | bytes 2097168 | tf_op jit(solution)/shard_map/while/body/eval_jaxpr/psum | solution.py:14
  349.5 8.9 multiply_subtract_fusion.2
  361.3 4.0 fusion.43
  365.4 55.6 %all-reduce.3.cloned.1.call-done = bf16[1024,512]{1,0:T(8,128)(2,1)} async-done(((bf16[1024,512]{1,0:T(8,128)(2,1)}), bf16[1024,512]{1,0:T(8,128)(2,1)}) %all-reduce.3.cloned.1.call-update) | async-done | bytes 1048592 | tf_op jit(solution)/shard_map/while/body/eval_jaxpr/psum | solution.py:14
  422.8 93.4 %all-reduce.5.cloned.1.call-done = bf16[512,2048]{1,0:T(8,128)(2,1)} async-done(((bf16[512,2048]{1,0:T(8,128)(2,1)}), bf16[512,2048]{1,0:T(8,128)(2,1)}) %all-reduce.5.cloned.1.call-update) | async-done | bytes 2097168 | tf_op jit(solution)/shard_map/while/body/eval_jaxpr/psum | solution.py:14
  516.2 8.9 multiply_subtract_fusion.2
  528.0 4.0 fusion.43
  532.0 55.4 %all-reduce.3.cloned.1.call-done = bf16[1024,512]{1,0:T(8,128)(2,1)} async-done(((bf16[1024,512]{1,0:T(8,128)(2,1)}), bf16[1024,512]{1,0:T(8,128)(2,1)}) %all-reduce.3.cloned.1.call-update) | async-done | bytes 1048592 | tf_op jit(solution)/shard_map/while/body/eval_jaxpr/psum | solution.py:14
  589.2 93.4 %all-reduce.5.cloned.1.call-done = bf16[512,2048]{1,0:T(8,128)(2,1)} async-done(((bf16[512,2048]{1,0:T(8,128)(2,1)}), bf16[512,2048]{1,0:T(8,128)(2,1)}) %all-reduce.5.cloned.1.call-update) | async-done | bytes 2097168 | tf_op jit(solution)/shard_map/while/body/eval_jaxpr/psum | solution.py:14
  682.6 8.9 multiply_subtract_fusion.2
  694.4 4.0 fusion.43
  698.5 55.6 %all-reduce.3.cloned.1.call-done = bf16[1024,512]{1,0:T(8,128)(2,1)} async-done(((bf16[1024,512]{1,0:T(8,128)(2,1)}), bf16[1024,512]{1,0:T(8,128)(2,1)}) %all-reduce.3.cloned.1.call-update) | async-done | bytes 1048592 | tf_op jit(solution)/shard_map/while/body/eval_jaxpr/psum | solution.py:14
  755.9 93.5 %all-reduce.5.cloned.1.call-done = bf16[512,2048]{1,0:T(8,128)(2,1)} async-done(((bf16[512,2048]{1,0:T(8,128)(2,1)}), bf16[512,2048]{1,0:T(8,128)(2,1)}) %all-reduce.5.cloned.1.call-update) | async-done | bytes 2097168 | tf_op jit(solution)/shard_map/while/body/eval_jaxpr/psum | solution.py:14
  849.4 8.9 multiply_subtract_fusion.2
  861.2 4.0 fusion.43
  865.3 55.6 %all-reduce.3.cloned.1.call-done = bf16[1024,512]{1,0:T(8,128)(2,1)} async-done(((bf16[1024,512]{1,0:T(8,128)(2,1)}), bf16[1024,512]{1,0:T(8,128)(2,1)}) %all-reduce.3.cloned.1.call-update) | async-done | bytes 1048592 | tf_op jit(solution)/shard_map/while/body/eval_jaxpr/psum | solution.py:14
  922.7 93.4 %all-reduce.5.cloned.1.call-done = bf16[512,2048]{1,0:T(8,128)(2,1)} async-done(((bf16[512,2048]{1,0:T(8,128)(2,1)}), bf16[512,2048]{1,0:T(8,128)(2,1)}) %all-reduce.5.cloned.1.call-update) | async-done | bytes 2097168 | tf_op jit(solution)/shard_map/while/body/eval_jaxpr/psum | solution.py:14
  1016.1 8.9 multiply_subtract_fusion.2
  1027.9 4.0 fusion.43
  1032.0 55.6 %all-reduce.3.cloned.1.call-done = bf16[1024,512]{1,0:T(8,128)(2,1)} async-done(((bf16[1024,512]{1,0:T(8,128)(2,1)}), bf16[1024,512]{1,0:T(8,128)(2,1)}) %all-reduce.3.cloned.1.call-update) | async-done | bytes 1048592 | tf_op jit(solution)/shard_map/while/body/eval_jaxpr/psum | solution.py:14
  1089.4 93.4 %all-reduce.5.cloned.1.call-done = bf16[512,2048]{1,0:T(8,128)(2,1)} async-done(((bf16[512,2048]{1,0:T(8,128)(2,1)}), bf16[512,2048]{1,0:T(8,128)(2,1)}) %all-reduce.5.cloned.1.call-update) | async-done | bytes 2097168 | tf_op jit(solution)/shard_map/while/body/eval_jaxpr/psum | solution.py:14
  1182.8 8.8 multiply_subtract_fusion.2
  1194.5 4.0 fusion.43
  1198.6 55.6 %all-reduce.3.cloned.1.call-done = bf16[1024,512]{1,0:T(8,128)(2,1)} async-done(((bf16[1024,512]{1,0:T(8,128)(2,1)}), bf16[1024,512]{1,0:T(8,128)(2,1)}) %all-reduce.3.cloned.1.call-update) | async-done | bytes 1048592 | tf_op jit(solution)/shard_map/while/body/eval_jaxpr/psum | solution.py:14
  1256.0 93.4 %all-reduce.5.cloned.1.call-done = bf16[512,2048]{1,0:T(8,128)(2,1)} async-done(((bf16[512,2048]{1,0:T(8,128)(2,1)}), bf16[512,2048]{1,0:T(8,128)(2,1)}) %all-reduce.5.cloned.1.call-update) | async-done | bytes 2097168 | tf_op jit(solution)/shard_map/while/body/eval_jaxpr/psum | solution.py:14
  1349.4 8.9 multiply_subtract_fusion.2
  1365.3 55.4 %all-reduce.3.cloned.1.call-done = bf16[1024,512]{1,0:T(8,128)(2,1)} async-done(((bf16[1024,512]{1,0:T(8,128)(2,1)}), bf16[1024,512]{1,0:T(8,128)(2,1)}) %all-reduce.3.cloned.1.call-update) | async-done | bytes 1048592 | tf_op jit(solution)/shard_map/while/body/eval_jaxpr/psum | solution.py:14
  1422.5 93.4 %all-reduce.5.cloned.1.call-done = bf16[512,2048]{1,0:T(8,128)(2,1)} async-done(((bf16[512,2048]{1,0:T(8,128)(2,1)}), bf16[512,2048]{1,0:T(8,128)(2,1)}) %all-reduce.5.cloned.1.call-update) | async-done | bytes 2097168 | tf_op jit(solution)/shard_map/while/body/eval_jaxpr/psum | solution.py:14
  1515.9 8.8 multiply_subtract_fusion.2
  1531.7 55.4 %all-reduce.3.cloned.1.call-done = bf16[1024,512]{1,0:T(8,128)(2,1)} async-done(((bf16[1024,512]{1,0:T(8,128)(2,1)}), bf16[1024,512]{1,0:T(8,128)(2,1)}) %all-reduce.3.cloned.1.call-update) | async-done | bytes 1048592 | tf_op jit(solution)/shard_map/while/body/eval_jaxpr/psum | solution.py:14
  1589.0 93.4 %all-reduce.5.cloned.1.call-done = bf16[512,2048]{1,0:T(8,128)(2,1)} async-done(((bf16[512,2048]{1,0:T(8,128)(2,1)}), bf16[512,2048]{1,0:T(8,128)(2,1)}) %all-reduce.5.cloned.1.call-update) | async-done | bytes 2097168 | tf_op jit(solution)/shard_map/while/body/eval_jaxpr/psum | solution.py:14
  1682.3 8.9 multiply_subtract_fusion.2
  1698.2 55.6 %all-reduce.3.cloned.1.call-done = bf16[1024,512]{1,0:T(8,128)(2,1)} async-done(((bf16[1024,512]{1,0:T(8,128)(2,1)}), bf16[1024,512]{1,0:T(8,128)(2,1)}) %all-reduce.3.cloned.1.call-update) | async-done | bytes 1048592 | tf_op jit(solution)/shard_map/while/body/eval_jaxpr/psum | solution.py:14
  1755.6 93.4 %all-reduce.5.cloned.1.call-done = bf16[512,2048]{1,0:T(8,128)(2,1)} async-done(((bf16[512,2048]{1,0:T(8,128)(2,1)}), bf16[512,2048]{1,0:T(8,128)(2,1)}) %all-reduce.5.cloned.1.call-update) | async-done | bytes 2097168 | tf_op jit(solution)/shard_map/while/body/eval_jaxpr/psum | solution.py:14
  1849.0 8.9 multiply_subtract_fusion.2
  1857.9 6.0 convert_element_type.98
  (101 shorter events, 64.5 us)
Async XLA Ops:
  10.0 39.8 %all-to-all-start = ((s32[128,2,1]{1,2,0:T(1,128)}), s32[128,2,1]{1,2,0:T(1,128)S(1)}, u32[]{:S(2)}, u32[]{:S(2)}) async-start(s32[128,2,1]{1,2,0:T(1,128)} %bitcast.3), calls=%async_computation | async-start | bytes 131072 | tf_op jit(solution)/shard_map/all_to_all | solution.py:38
  49.8 110.1 %all-to-all-start.1 = ((bf16[256,128,128]{2,1,0:T(8,128)(2,1)}), bf16[256,128,128]{2,1,0:T(8,128)(2,1)}, u32[]{:S(2)}, u32[]{:S(2)}) async-start(bf16[256,128,128]{2,1,0:T(8,128)(2,1)} %scatter_fusion), calls=%async_computation.1 | async-start | bytes 16777216 | tf_op jit(solution)/shard_map/all_to_all | solution.py:37
  172.5 6.4 copy-start
  178.9 7.8 copy-start.1
  178.9 7.8 copy-start.2
  178.9 7.7 copy-start.3
  186.7 67.5 %all-reduce.3.cloned.1.call-start = ((), (), s32[]{:S(2)}) async-start(), calls=%async_computation.2 | async-start | bytes 2097152 | tf_op jit(solution)/shard_map/while/body/eval_jaxpr/psum | solution.py:14
  189.6 159.9 %all-reduce.5.cloned.1.call-start = ((), (), s32[]{:S(2)}) async-start(), calls=%async_computation.3 | async-start | bytes 4194304 | tf_op jit(solution)/shard_map/while/body/eval_jaxpr/psum | solution.py:14
  358.4 62.6 %all-reduce.3.cloned.1.call-start = ((), (), s32[]{:S(2)}) async-start(), calls=%async_computation.2 | async-start | bytes 2097152 | tf_op jit(solution)/shard_map/while/body/eval_jaxpr/psum | solution.py:14
  361.2 154.9 %all-reduce.5.cloned.1.call-start = ((), (), s32[]{:S(2)}) async-start(), calls=%async_computation.3 | async-start | bytes 4194304 | tf_op jit(solution)/shard_map/while/body/eval_jaxpr/psum | solution.py:14
  525.0 62.4 %all-reduce.3.cloned.1.call-start = ((), (), s32[]{:S(2)}) async-start(), calls=%async_computation.2 | async-start | bytes 2097152 | tf_op jit(solution)/shard_map/while/body/eval_jaxpr/psum | solution.py:14
  527.9 154.7 %all-reduce.5.cloned.1.call-start = ((), (), s32[]{:S(2)}) async-start(), calls=%async_computation.3 | async-start | bytes 4194304 | tf_op jit(solution)/shard_map/while/body/eval_jaxpr/psum | solution.py:14
  691.5 62.6 %all-reduce.3.cloned.1.call-start = ((), (), s32[]{:S(2)}) async-start(), calls=%async_computation.2 | async-start | bytes 2097152 | tf_op jit(solution)/shard_map/while/body/eval_jaxpr/psum | solution.py:14
  694.3 155.1 %all-reduce.5.cloned.1.call-start = ((), (), s32[]{:S(2)}) async-start(), calls=%async_computation.3 | async-start | bytes 4194304 | tf_op jit(solution)/shard_map/while/body/eval_jaxpr/psum | solution.py:14
  858.3 62.6 %all-reduce.3.cloned.1.call-start = ((), (), s32[]{:S(2)}) async-start(), calls=%async_computation.2 | async-start | bytes 2097152 | tf_op jit(solution)/shard_map/while/body/eval_jaxpr/psum | solution.py:14
  861.1 155.0 %all-reduce.5.cloned.1.call-start = ((), (), s32[]{:S(2)}) async-start(), calls=%async_computation.3 | async-start | bytes 4194304 | tf_op jit(solution)/shard_map/while/body/eval_jaxpr/psum | solution.py:14
  1025.0 62.6 %all-reduce.3.cloned.1.call-start = ((), (), s32[]{:S(2)}) async-start(), calls=%async_computation.2 | async-start | bytes 2097152 | tf_op jit(solution)/shard_map/while/body/eval_jaxpr/psum | solution.py:14
  1027.8 154.9 %all-reduce.5.cloned.1.call-start = ((), (), s32[]{:S(2)}) async-start(), calls=%async_computation.3 | async-start | bytes 4194304 | tf_op jit(solution)/shard_map/while/body/eval_jaxpr/psum | solution.py:14
  1191.6 62.6 %all-reduce.3.cloned.1.call-start = ((), (), s32[]{:S(2)}) async-start(), calls=%async_computation.2 | async-start | bytes 2097152 | tf_op jit(solution)/shard_map/while/body/eval_jaxpr/psum | solution.py:14
  1194.5 154.9 %all-reduce.5.cloned.1.call-start = ((), (), s32[]{:S(2)}) async-start(), calls=%async_computation.3 | async-start | bytes 4194304 | tf_op jit(solution)/shard_map/while/body/eval_jaxpr/psum | solution.py:14
  1358.3 62.4 %all-reduce.3.cloned.1.call-start = ((), (), s32[]{:S(2)}) async-start(), calls=%async_computation.2 | async-start | bytes 2097152 | tf_op jit(solution)/shard_map/while/body/eval_jaxpr/psum | solution.py:14
  1361.1 154.7 %all-reduce.5.cloned.1.call-start = ((), (), s32[]{:S(2)}) async-start(), calls=%async_computation.3 | async-start | bytes 4194304 | tf_op jit(solution)/shard_map/while/body/eval_jaxpr/psum | solution.py:14
  1524.7 62.4 %all-reduce.3.cloned.1.call-start = ((), (), s32[]{:S(2)}) async-start(), calls=%async_computation.2 | async-start | bytes 2097152 | tf_op jit(solution)/shard_map/while/body/eval_jaxpr/psum | solution.py:14
  1527.6 154.7 %all-reduce.5.cloned.1.call-start = ((), (), s32[]{:S(2)}) async-start(), calls=%async_computation.3 | async-start | bytes 4194304 | tf_op jit(solution)/shard_map/while/body/eval_jaxpr/psum | solution.py:14
  1691.2 62.6 %all-reduce.3.cloned.1.call-start = ((), (), s32[]{:S(2)}) async-start(), calls=%async_computation.2 | async-start | bytes 2097152 | tf_op jit(solution)/shard_map/while/body/eval_jaxpr/psum | solution.py:14
  1694.0 155.0 %all-reduce.5.cloned.1.call-start = ((), (), s32[]{:S(2)}) async-start(), calls=%async_computation.3 | async-start | bytes 4194304 | tf_op jit(solution)/shard_map/while/body/eval_jaxpr/psum | solution.py:14
Sparse Core Ops, SparseCore 0:
  189.8 64.2 all-reduce.2
  257.5 91.9 all-reduce.4
  361.5 59.3 all-reduce.2
  424.1 91.9 all-reduce.4
  528.0 59.3 all-reduce.2
  590.6 91.9 all-reduce.4
  694.6 59.3 all-reduce.2
  757.4 91.9 all-reduce.4
  861.4 59.3 all-reduce.2
  924.0 92.0 all-reduce.4
  1028.1 59.3 all-reduce.2
  1090.7 91.9 all-reduce.4
  1194.8 59.3 all-reduce.2
  1257.4 91.9 all-reduce.4
  1361.2 59.3 all-reduce.2
  1423.8 91.9 all-reduce.4
  1527.7 59.3 all-reduce.2
  1590.3 91.9 all-reduce.4
  1694.3 59.3 all-reduce.2
  1756.9 92.0 all-reduce.4
where the time goes:
time: 1880 us; the launch traced here: 1870 us
  waiting for transfers between devices  1590 us (85%)
  matrix products  113 us (6%)
  other arithmetic  89.1 us (5%)
  local copies, waits for them, and re-layouts  39.8 us (2%)
  starting transfers between devices  20.6 us (1%)
    psum x20, waiting for transfers between devices, broadcast(): return lax.psum(block, axis)  1490 us
    all_to_all x1, waiting for transfers between devices, shards(): lax.all_to_all(send_tiles, ('row', 'col'), split_axis=0, concat_axis=0, t...  98.4 us
    dot_general x10, matrix products, panel_step(): product = jnp.dot(left, right, preferred_element_type=jnp.float32)  88.5 us
    select_n x20, other arithmetic, broadcast(): jnp.where(lax.axis_index(axis) == owner, block, jnp.zeros_like(block))  68.2 us
  transfers between devices with their start and end apart: 22, of which 21 were waited for; matrix products, arithmetic and copies ran while one was open for 5% of the time, Pallas kernels for 0%

commit v1 on v0

v1 whole, which is shorter than its diff:
```python
import functools

import jax
import jax.numpy as jnp
from jax import lax
from jax.experimental import pallas as pl
from jax.experimental.pallas import tpu as pltpu
from jax.sharding import PartitionSpec as P

PB = 512
SK = 128
TILE = 128
PANELS = 10
CAP = 2
ND = 128
NR = 16
NC = 8
ROWS = 1024
COLS = 2048
RANK = PANELS * SK
RSRC = 5
CSRC = 3
MESH = pl.DeviceIdType.MESH
MIB = 2**20


def div(a, b):
    return lax.div(a, jnp.int32(b))


def rem(a, b):
    return lax.rem(a, jnp.int32(b))


def partner(me, step):
    j = rem(step * 31, 128)
    bit = lambda p: rem(div(j, 2**p), 2)
    dx = bit(5) * 2 + bit(2)
    dz = bit(0) * 2 + bit(1)
    dy = bit(6) * 2 + bit(4)
    dk = bit(3)
    x = rem(div(me, 32) + dx, 4)
    z = rem(div(me, 8) + dz, 4)
    y = rem(div(me, 2) + dy, 4)
    k = rem(me + dk, 2)
    return x * 32 + z * 8 + y * 2 + k


def exchange_kernel(
    idx_ref, slot_ref, tiles_ref, got_ref, gslot_ref, send, held, lsem, ssem, rsem, slot_ssem, slot_rsem
):
    me = lax.axis_index("row") * NC + lax.axis_index("col")
    load = pltpu.make_async_copy(tiles_ref, held, lsem.at[0])
    load.start()
    barrier = pltpu.get_barrier_semaphore()

    def greet(step, carry):
        p = partner(me, step)
        pl.semaphore_signal(barrier, inc=1, device_id=(div(p, NC), rem(p, NC)), device_id_type=MESH)
        return carry

    lax.fori_loop(1, ND, greet, 0)
    own_slot = pltpu.make_async_copy(slot_ref.at[me], gslot_ref.at[me], lsem.at[1])
    own_slot.start()
    load.wait()

    def pack(p):
        for k in range(CAP):
            send[p, k] = held[idx_ref[k, p]]

    pack(me)
    own = pltpu.make_async_copy(send.at[me], got_ref.at[me], lsem.at[2])
    own.start()
    pl.semaphore_wait(barrier, ND - 1)

    def copies(p, landing):
        device = (div(p, NC), rem(p, NC))
        tile = pltpu.make_async_remote_copy(
            src_ref=send.at[p], dst_ref=got_ref.at[landing], send_sem=ssem.at[p], recv_sem=rsem.at[landing],
            device_id=device, device_id_type=MESH,
        )
        slot = pltpu.make_async_remote_copy(
            src_ref=slot_ref.at[p], dst_ref=gslot_ref.at[landing], send_sem=slot_ssem.at[p],
            recv_sem=slot_rsem.at[landing], device_id=device, device_id_type=MESH,
        )
        return tile, slot

    def post(step, carry):
        p = partner(me, step)
        pack(p)
        tile, slot = copies(p, me)
        tile.start()
        slot.start()
        return carry

    lax.fori_loop(1, ND, post, 0)

    def finish(step, carry):
        p = partner(me, step)
        tile, slot = copies(p, p)
        tile.wait()
        slot.wait()
        return carry

    lax.fori_loop(1, ND, finish, 0)
    own_slot.wait()
    own.wait()


def exchange(idx, slots, tiles):
    any_spec = pl.BlockSpec(memory_space=pl.ANY)
    return pl.pallas_call(
        exchange_kernel,
        out_shape=(
            jax.ShapeDtypeStruct((ND, CAP, TILE, TILE), jnp.bfloat16),
            jax.ShapeDtypeStruct((ND, 1, TILE), jnp.int32),
        ),
        in_specs=[pl.BlockSpec(memory_space=pltpu.SMEM), any_spec, any_spec],
        out_specs=(any_spec, any_spec),
        scratch_shapes=[
            pltpu.VMEM((ND, CAP, TILE, TILE), jnp.bfloat16),
            pltpu.VMEM((ND, TILE, TILE), jnp.bfloat16),
            pltpu.SemaphoreType.DMA((3,)),
            pltpu.SemaphoreType.DMA((ND,)),
            pltpu.SemaphoreType.DMA((ND,)),
            pltpu.SemaphoreType.DMA((ND,)),
            pltpu.SemaphoreType.DMA((ND,)),
        ],
        compiler_params=pltpu.CompilerParams(
            collective_id=0, has_side_effects=True, vmem_limit_bytes=32 * MIB
        ),
        name="tile_exchange",
    )(idx, slots, tiles)


CHUNK = 8


def assemble_kernel(
    slot_ref, front_ref, got_ref, omega_ref, psi_ref, grid_ref, b_ref, s_ref, t_ref, grid, front, got, fsem, gsem, osem
):
    r = lax.axis_index("row")
    c = lax.axis_index("col")
    n_chunks = ND // CHUNK
    load_front = pltpu.make_async_copy(front_ref, front, fsem)
    load_front.start()
    loads = [
        pltpu.make_async_copy(got_ref.at[pl.ds(i * CHUNK, CHUNK)], got.at[pl.ds(i * CHUNK, CHUNK)], gsem.at[i])
        for i in range(n_chunks)
    ]
    for load in loads:
        load.start()
    load_front.wait()

    def widen(i, carry):
        rows = pl.ds(pl.multiple_of(i * 64, 64), 64)
        grid[rows, :] = front[rows, :].astype(jnp.float32)
        return carry

    lax.fori_loop(0, ROWS // 64, widen, 0)

    def add(source, carry):
        @pl.when(rem(source, CHUNK) == 0)
        def _():
            chunk = div(source, CHUNK)
            pltpu.make_async_copy(
                got_ref.at[pl.ds(source, CHUNK)], got.at[pl.ds(source, CHUNK)], gsem.at[chunk]
            ).wait()

        for k in range(CAP):
            slot = slot_ref[source, k]

            @pl.when(slot >= 0)
            def _():
                rows = pl.ds(pl.multiple_of(div(slot, COLS // TILE) * TILE, TILE), TILE)
                cols = pl.ds(pl.multiple_of(rem(slot, COLS // TILE) * TILE, TILE), TILE)
                grid[rows, cols] += got[source, k].astype(jnp.float32)

        return carry

    lax.fori_loop(0, ND, add, 0)
    store = pltpu.make_async_copy(grid, grid_ref, osem)
    store.start()

    @pl.when(c < CSRC)
    def _():
        def rows_of(i, carry):
            rows = pl.ds(pl.multiple_of(i * 256, 256), 256)
            for k in range(4):
                block = grid[rows, k * PB : (k + 1) * PB].astype(jnp.bfloat16)
                b_ref[rows, k * SK : (k + 1) * SK] = jnp.dot(
                    block, omega_ref[...], preferred_element_type=jnp.float32
                ).astype(jnp.bfloat16)
            return carry

        lax.fori_loop(0, ROWS // 256, rows_of, 0)

    @pl.when(r < RSRC)
    def _():
        psi_t = psi_ref[...].T
        for j in range(2):
            def cols_of(i, carry):
                cols = pl.ds(pl.multiple_of(i * 512, 512), 512)
                block = grid[j * PB : (j + 1) * PB, cols].astype(jnp.bfloat16)
                s_ref[j * SK : (j + 1) * SK, cols] = jnp.dot(
                    psi_t, block, preferred_element_type=jnp.float32
                ).astype(jnp.bfloat16)
                return carry

            lax.fori_loop(0, COLS // 512, cols_of, 0)

        @pl.when(c < CSRC)
        def _():
            for j in range(2):
                t_ref[j * SK : (j + 1) * SK, :] = jnp.dot(
                    psi_t, b_ref[j * PB : (j + 1) * PB, :], preferred_element_type=jnp.float32
                ).astype(jnp.bfloat16)

    store.wait()


def assemble(slots, front, got, omega, psi):
    any_spec = pl.BlockSpec(memory_space=pl.ANY)
    vmem = pl.BlockSpec(memory_space=pltpu.VMEM)
    return pl.pallas_call(
        assemble_kernel,
        out_shape=(
            jax.ShapeDtypeStruct((ROWS, COLS), jnp.float32),
            jax.ShapeDtypeStruct((ROWS, 4 * SK), jnp.bfloat16),
            jax.ShapeDtypeStruct((2 * SK, COLS), jnp.bfloat16),
            jax.ShapeDtypeStruct((2 * SK, 4 * SK), jnp.bfloat16),
        ),
        in_specs=[pl.BlockSpec(memory_space=pltpu.SMEM), any_spec, any_spec, vmem, vmem],
        out_specs=(any_spec, vmem, vmem, vmem),
        scratch_shapes=[
            pltpu.VMEM((ROWS, COLS), jnp.float32),
            pltpu.VMEM((ROWS, COLS), jnp.bfloat16),
            pltpu.VMEM((ND, CAP, TILE, TILE), jnp.bfloat16),
            pltpu.SemaphoreType.DMA,
            pltpu.SemaphoreType.DMA((ND // CHUNK,)),
            pltpu.SemaphoreType.DMA,
        ],
        compiler_params=pltpu.CompilerParams(vmem_limit_bytes=40 * MIB),
        name="extend_add",
    )(slots, front, got, omega, psi)


TR = 2 * SK // NC


def gather_kernel(
    b_ref, s_ref, t_ref, ball, sall, tall,
    lsem, t1s, t1r, t2s, t2r, t3s, t3r, bss, bsr, bas, bar, sss, ssr, sas, sar,
):
    r = lax.axis_index("row")
    c = lax.axis_index("col")
    x, z = div(r, 4), rem(r, 4)
    y, k = div(c, 2), rem(c, 2)

    barrier = pltpu.get_barrier_semaphore()
    for i in range(1, NR):
        pl.semaphore_signal(barrier, inc=1, device_id=(rem(r + i, NR), c), device_id_type=MESH)
    for i in range(1, NC):
        pl.semaphore_signal(barrier, inc=1, device_id=(r, rem(c + i, NC)), device_id_type=MESH)
    pl.semaphore_wait(barrier, NR - 1 + NC - 1)

    def remote(src, dst, send, recv, device):
        return pltpu.make_async_remote_copy(
            src_ref=src, dst_ref=dst, send_sem=send, recv_sem=recv, device_id=device, device_id_type=MESH
        )

    def t1(cc, src_c, width, sem):
        return remote(
            t_ref.at[pl.ds(pl.multiple_of(cc * TR, TR), TR), pl.ds(0, width)],
            tall.at[cc, r, :, pl.ds(src_c * 4 * SK, width)],
            t1s.at[sem], t1r.at[src_c], (r, cc),
        )

    def b1(cc, src_c, width, sem):
        return remote(
            b_ref.at[pl.ds(pl.multiple_of(cc * TILE, TILE), TILE), pl.ds(0, width)],
            ball.at[cc, :, pl.ds(src_c * 4 * SK, width)],
            bss.at[sem], bsr.at[src_c], (r, cc),
        )

    def s1(rr, sem):
        return remote(
            s_ref.at[:, pl.ds(pl.multiple_of(rr * TILE, TILE), TILE)], sall.at[rr, r],
            sss.at[sem], ssr.at[r], (rr, c),
        )

    widths = [4 * SK, 4 * SK, 2 * SK]

    def own_t(src_c):
        w = widths[src_c]
        return pltpu.make_async_copy(
            t_ref.at[pl.ds(pl.multiple_of(c * TR, TR), TR), pl.ds(0, w)],
            tall.at[c, r, :, pl.ds(src_c * 4 * SK, w)], lsem.at[0],
        )

    def own_b(src_c):
        w = widths[src_c]
        return pltpu.make_async_copy(
            b_ref.at[pl.ds(pl.multiple_of(c * TILE, TILE), TILE), pl.ds(0, w)],
            ball.at[c, :, pl.ds(src_c * 4 * SK, w)], lsem.at[1],
        )

    def own_s():
        return pltpu.make_async_copy(
            s_ref.at[:, pl.ds(pl.multiple_of(r * TILE, TILE), TILE)], sall.at[r, r], lsem.at[2]
        )

    @pl.when(r < RSRC)
    def _():
        for src_c in range(CSRC):
            @pl.when(c == src_c)
            def _():
                own_t(src_c).start()
                for i in range(1, NC):
                    t1(rem(c + i, NC), src_c, widths[src_c], i).start()

    for src_c in range(CSRC):
        @pl.when(c == src_c)
        def _():
            own_b(src_c).start()
            for i in range(1, NC):
                b1(rem(c + i, NC), src_c, widths[src_c], i).start()

    @pl.when(r < RSRC)
    def _():
        own_s().start()
        for i in range(1, NR):
            s1(rem(r + i, NR), i).start()

    def t2(src_r, rr, sem):
        return remote(tall.at[c, src_r], tall.at[c, src_r], t2s.at[sem], t2r.at[src_r], (rr, c))

    @pl.when(r < RSRC)
    def _():
        for src_c in range(CSRC):
            @pl.when(c != src_c)
            def _():
                t1(c, src_c, widths[src_c], 0).wait_recv()

            @pl.when(c == src_c)
            def _():
                own_t(src_c).wait()
        for i in range(1, NR):
            t2(r, rem(r + i, NR), i).start()

    def along(axis, d):
        if axis == "x":
            return rem(x + d, 4) * 4 + z
        return x * 4 + rem(z + d, 4)

    def s2(half, piece, rr, sem):
        part = sall.at[piece, :, pl.ds(half * SK, SK), :]
        return remote(part, part, sas.at[half, sem], sar.at[half, piece], (rr, c))

    for src_r in range(RSRC):
        @pl.when(r != src_r)
        def _():
            remote(
                s_ref.at[:, pl.ds(0, TILE)], sall.at[r, src_r], sss.at[0], ssr.at[src_r], (r, c)
            ).wait_recv()

        @pl.when(r == src_r)
        def _():
            own_s().wait()

    axes = (("x", "z"), ("z", "x"))
    order = (1, 3, 2)
    for n, d in enumerate(order):
        for half in range(2):
            s2(half, r, along(axes[half][0], d), n).start()

    def t3(piece, cc, sem):
        return remote(tall.at[piece], tall.at[piece], t3s.at[sem], t3r.at[piece], (r, cc))

    def b3(piece, cc, sem):
        return remote(ball.at[piece], ball.at[piece], bas.at[sem], bar.at[piece], (r, cc))

    for src_r in range(RSRC):
        @pl.when(r != src_r)
        def _():
            t2(src_r, r, 0).wait_recv()
    other = y * 2 + (1 - k)
    for n, d in enumerate(order):
        t3(c, rem(y + d, 4) * 2 + k, n).start()
    t3(c, other, 3).start()

    for n, d in enumerate(order):
        for half in range(2):
            s2(half, r, along(axes[half][1], d), 3 + n).start()

    for src_c in range(CSRC):
        @pl.when(c != src_c)
        def _():
            b1(c, src_c, widths[src_c], 0).wait_recv()

        @pl.when(c == src_c)
        def _():
            own_b(src_c).wait()
    for n, d in enumerate(order):
        b3(c, rem(y + d, 4) * 2 + k, n).start()
    b3(c, other, 3).start()

    for m, dd in enumerate(order):
        for half in range(2):
            piece = along(axes[half][0], dd)
            s2(half, piece, r, 0).wait_recv()
            for n, d in enumerate(order):
                s2(half, piece, along(axes[half][1], d), 6 + 3 * m + n).start()
    for m, dd in enumerate(order):
        piece = rem(y + dd, 4) * 2 + k
        t3(piece, c, 0).wait_recv()
        t3(piece, other, 4 + m).start()
    for m, dd in enumerate(order):
        piece = rem(y + dd, 4) * 2 + k
        b3(piece, c, 0).wait_recv()
        b3(piece, other, 4 + m).start()

    for yy in range(4):
        piece = yy * 2 + (1 - k)
        t3(piece, c, 0).wait_recv()
        b3(piece, c, 0).wait_recv()
    for dd in (1, 3, 2):
        for half in range(2):
            first, second = axes[half]
            for d in range(4):
                if first == "x":
                    piece = rem(x + d, 4) * 4 + rem(z + dd, 4)
                else:
                    piece = rem(x + dd, 4) * 4 + rem(z + d, 4)
                s2(half, piece, r, 0).wait_recv()

    @pl.when(r < RSRC)
    def _():
        for src_c in range(CSRC):
            @pl.when(c == src_c)
            def _():
                for i in range(1, NC):
                    t1(rem(c + i, NC), src_c, widths[src_c], i).wait_send()
        for i in range(1, NR):
            s1(rem(r + i, NR), i).wait_send()
            t2(r, rem(r + i, NR), i).wait_send()

    for src_c in range(CSRC):
        @pl.when(c == src_c)
        def _():
            for i in range(1, NC):
                b1(rem(c + i, NC), src_c, widths[src_c], i).wait_send()
    for i in range(7):
        t3(c, other, i).wait_send()
        b3(c, other, i).wait_send()
    for half in range(2):
        for i in range(15):
            s2(half, r, rem(r + 1, NR), i).wait_send()


def gather(b, s, t):
    any_spec = pl.BlockSpec(memory_space=pl.ANY)
    dma = pltpu.SemaphoreType.DMA
    return pl.pallas_call(
        gather_kernel,
        out_shape=(
            jax.ShapeDtypeStruct((NC, TILE, RANK), jnp.bfloat16),
            jax.ShapeDtypeStruct((NR, RSRC, 2 * SK, TILE), jnp.bfloat16),
            jax.ShapeDtypeStruct((NC, RSRC, TR, RANK), jnp.bfloat16),
        ),
        in_specs=[any_spec] * 3,
        out_specs=(any_spec,) * 3,
        scratch_shapes=[
            dma((3,)),
            dma((NC,)), dma((CSRC,)), dma((NR,)), dma((RSRC,)), dma((7,)), dma((NC,)),
            dma((NC,)), dma((CSRC,)), dma((7,)), dma((NC,)),
            dma((NR,)), dma((RSRC,)), dma((2, 15)), dma((2, NR)),
        ],
        compiler_params=pltpu.CompilerParams(collective_id=1, has_side_effects=True),
        name="sketch_gather",
    )(b, s, t)


UR = 256


def update_kernel(
    ball_ref, sall_ref, tall_ref, core_ref, grid_ref, out_ref,
    ball, sall, tall, state, left, right, wmat, vmat, gbuf, obuf, lsem, ssem, tsem, gsem, osem,
):
    r = lax.axis_index("row")
    c = lax.axis_index("col")
    f32 = jnp.float32
    bf16 = jnp.bfloat16
    t_loads = [
        pltpu.make_async_copy(tall_ref.at[cc], tall.at[:, pl.ds(cc * TR, TR), :], tsem.at[cc]) for cc in range(NC)
    ]
    for load in t_loads:
        load.start()
    b_load = pltpu.make_async_copy(ball_ref, ball, lsem)
    b_load.start()
    s_loads = [
        pltpu.make_async_copy(sall_ref.at[p], sall.at[:, :, pl.ds(p * TILE, TILE)], ssem.at[p]) for p in range(NR)
    ]
    for load in s_loads:
        load.start()
    g_loads = [
        pltpu.make_async_copy(grid_ref.at[pl.ds(i * UR, UR)], gbuf.at[i], gsem.at[i]) for i in range(ROWS // UR)
    ]
    for load in g_loads:
        load.start()
    for load in t_loads:
        load.wait()
    core = core_ref[...]

    for q in range(RSRC):
        state[q * 256 : (q + 1) * 256, :] = tall[q].astype(f32)
    for s in range(PANELS - 1):
        lo, hi = s * SK, (s + 1) * SK
        wmat[lo:hi, hi:] = state[lo:hi, hi:].astype(bf16)
        vmat[hi:, lo:hi] = jnp.dot(state[hi:, lo:hi].astype(bf16), core, preferred_element_type=f32).astype(bf16)
        if s < PANELS - 2:
            state[hi:, hi:] -= jnp.dot(vmat[hi:, lo:hi], wmat[lo:hi, hi:], preferred_element_type=f32)

    b_load.wait()
    for s in range(PANELS):
        lo, hi = s * SK, (s + 1) * SK

        def left_rows(i, carry):
            rows = pl.ds(pl.multiple_of(i * 512, 512), 512)
            basis = ball[rows, lo:hi].astype(f32)
            if s:
                basis -= jnp.dot(left[rows, :lo], wmat[:lo, lo:hi], preferred_element_type=f32)
            left[rows, lo:hi] = jnp.dot(basis.astype(bf16), core, preferred_element_type=f32).astype(bf16)
            return carry

        lax.fori_loop(0, ROWS // 512, left_rows, 0)

    for load in s_loads:
        load.wait()
    for s in range(PANELS):
        lo, hi = s * SK, (s + 1) * SK

        def right_cols(i, carry):
            cols = pl.ds(pl.multiple_of(i * 512, 512), 512)
            block = sall[s // 2, (s % 2) * SK : (s % 2 + 1) * SK, cols].astype(f32)
            if s:
                block -= jnp.dot(vmat[lo:hi, :lo], right[:lo, cols], preferred_element_type=f32)
            right[lo:hi, cols] = block.astype(bf16)
            return carry

        lax.fori_loop(0, COLS // 512, right_cols, 0)

    @pl.when(r < RSRC)
    def _():
        row_pos = r * ROWS + lax.broadcasted_iota(jnp.int32, (ROWS, SK), 0)
        for s in range(PANELS):
            block = left[:, s * SK : (s + 1) * SK]
            left[:, s * SK : (s + 1) * SK] = jnp.where(row_pos >= (s + 1) * PB, block, jnp.zeros_like(block))

    @pl.when(c < CSRC)
    def _():
        col_pos = c * COLS + lax.broadcasted_iota(jnp.int32, (SK, COLS), 1)
        for s in range(PANELS):
            block = right[s * SK : (s + 1) * SK, :]
            right[s * SK : (s + 1) * SK, :] = jnp.where(col_pos >= (s + 1) * PB, block, jnp.zeros_like(block))

    stores = []
    for i in range(ROWS // UR):
        g_loads[i].wait()
        rows = slice(i * UR, (i + 1) * UR)

        def cols_of(q, carry):
            cols = pl.ds(pl.multiple_of(q * 512, 512), 512)
            product = jnp.dot(left[rows, :], right[:, cols], preferred_element_type=f32)
            obuf[i, :, cols] = (gbuf[i, :, cols] - product).astype(bf16)
            return carry

        lax.fori_loop(0, COLS // 512, cols_of, 0)
        store = pltpu.make_async_copy(obuf.at[i], out_ref.at[pl.ds(i * UR, UR)], osem.at[i])
        store.start()
        stores.append(store)
    for store in stores:
        store.wait()


def update(ball, sall, tall, core, grid):
    any_spec = pl.BlockSpec(memory_space=pl.ANY)
    vmem = pl.BlockSpec(memory_space=pltpu.VMEM)
    dma = pltpu.SemaphoreType.DMA
    bf16 = jnp.bfloat16
    n = ROWS // UR
    return pl.pallas_call(
        update_kernel,
        out_shape=jax.ShapeDtypeStruct((ROWS, COLS), bf16),
        in_specs=[any_spec, any_spec, any_spec, vmem, any_spec],
        out_specs=any_spec,
        scratch_shapes=[
            pltpu.VMEM((ROWS, RANK), bf16),
            pltpu.VMEM((RSRC, 2 * SK, COLS), bf16),
            pltpu.VMEM((RSRC, 2 * SK, RANK), bf16),
            pltpu.VMEM((RANK, RANK), jnp.float32),
            pltpu.VMEM((ROWS, RANK), bf16),
            pltpu.VMEM((RANK, COLS), bf16),
            pltpu.VMEM((RANK, RANK), bf16),
            pltpu.VMEM((RANK, RANK), bf16),
            pltpu.VMEM((n, UR, COLS), jnp.float32),
            pltpu.VMEM((n, UR, COLS), bf16),
            dma, dma((NR,)), dma((NC,)), dma((n,)), dma((n,)),
        ],
        compiler_params=pltpu.CompilerParams(vmem_limit_bytes=56 * MIB),
        name="panel_update",
    )(ball, sall, tall, core, grid)


def shards(front, tiles, counts, dest_owner, dest_slot, omega, psi, core):
    owners = dest_owner[:, 0]
    strip = jnp.arange(ND, dtype=jnp.int32)
    same = owners[:, None] == owners[None, :]
    before = strip[None, :] < strip[:, None]
    ranks = jnp.sum((same & before).astype(jnp.int32), axis=1)
    valid = strip < counts[0]
    named = strip[None, :, None] == owners[None, None, :]
    hit = named & (ranks[None, None, :] == jnp.arange(CAP, dtype=jnp.int32)[:, None, None])
    idx = jnp.sum(jnp.where(hit, strip[None, None, :], 0), axis=2)
    slots = jnp.sum(jnp.where(hit & valid[None, None, :], dest_slot[None, None, :] + 1, 0), axis=2) - 1
    slots = jnp.pad(slots.T[:, None, :], ((0, 0), (0, 0), (0, TILE - CAP)))
    got, got_slots = exchange(idx, slots, tiles)
    grid, b, s, t = assemble(got_slots[:, 0, :], front, got, omega, psi)
    ball, sall, tall = gather(b, s, t)
    return update(ball.reshape(ROWS, RANK), sall, tall, core, grid)


def solution(mesh):
    in_specs = (
        P("row", "col"),
        P(("row", "col"), None, None),
        P(("row", "col")),
        P(("row", "col"), None),
        P(("row", "col")),
        P(),
        P(),
        P(),
    )
    out_specs = P("row", "col")
    return jax.shard_map(shards, mesh=mesh, in_specs=in_specs, out_specs=out_specs, check_vma=False)
```

time: 1880 us -> 253 us (0.13)
  the two profiles are of different devices: /device:TPU:80 before, /device:TPU:97 now
where the time goes in v1:
time: 253 us; the launch traced here: 252 us
  Pallas kernels  240 us (95%)
  local copies, waits for them, and re-layouts  9.29 us (4%)
    pallas_call x1, Pallas kernels, exchange(): pl.pallas_call(exchange_kernel, out_shape=(jax.ShapeDtypeStruct((ND, CAP,...  116 us
    pallas_call x1, Pallas kernels, gather(): pl.pallas_call(gather_kernel, out_shape=(jax.ShapeDtypeStruct((NC, TILE,...  73.3 us
    pallas_call x1, Pallas kernels, update(): pl.pallas_call(update_kernel, out_shape=jax.ShapeDtypeStruct((ROWS, COLS)...  39 us
    pallas_call x1, Pallas kernels, assemble(): pl.pallas_call(assemble_kernel, out_shape=(jax.ShapeDtypeStruct((ROWS, CO...  11.7 us
    unnamed x16, local copies, waits for them, and re-layouts  9.13 us

profile of v1, /device:TPU:97, one launch (start us, length us, event | category | flops | bytes accessed | tf_op | source)
XLA Modules:
  0.0 252.5 jit_solution(8509648029806110210)
XLA Ops:
  0.7 0.9 convert_reduce_fusion
  1.6 0.7 broadcast_add_fusion.1
  2.2 0.7 iota_compare_fusion.1
  2.9 0.2 select_reduce_fusion
  3.1 0.1 copy.11
  3.2 0.0 copy-start.1
  3.3 0.0 copy-start.2
  3.3 2.3 copy-done.2
  5.6 0.0 copy-start.6
  5.6 115.8 %tile_exchange.1 = (bf16[128,2,128,128]{3,2,1,0:T(8,128)(2,1)S(1)}, s32[128,1,128]{2,1,0:T(1,128)S(1)}) custom-call(s32[2,128]{1,0:T(2,128)S(1)} %get-tuple-element.24.idx_ref, s32[128,1,128]{2,1,0:T(1,128)S(1)} %pad.4.slot_ref, bf16[128,128,128]{2,1,0:T(8,128)(2,1)S(1)} %copy-done.2), custom_call_target="tpu_custom_call" | custom-call | tf_op jit(solution)/shard_map/tile_exchange/pallas_call | solution.py:112
  121.4 0.0 copy-start
  121.4 3.2 %copy-done = bf16[128,2,128,128]{3,2,1,0:T(8,128)(2,1)} copy-done((bf16[128,2,128,128]{3,2,1,0:T(8,128)(2,1)}, bf16[128,2,128,128]{3,2,1,0:T(8,128)(2,1)S(1)}, u32[]{:S(2)}) %copy-start) | copy-done | bytes 8388632
  124.6 0.0 copy-done.1
  124.7 0.0 copy-done.6
  124.7 0.0 copy-start.7
  124.7 0.9 copy-done.7
  125.6 11.7 %extend_add.1 = (f32[1024,2048]{1,0:T(8,128)}, bf16[1024,512]{1,0:T(8,128)(2,1)S(1)}, bf16[256,2048]{1,0:T(8,128)(2,1)S(1)}, bf16[256,512]{1,0:T(8,128)(2,1)S(1)}) custom-call(s32[128,128]{1,0:T(8,128)S(1)} %bitcast.8, bf16[1024,2048]{1,0:T(8,128)(2,1)S(1)} %copy-done.1, bf16[128,2,128,128]{3,2,1,0:T(8,128)(2,1)} %copy-done, bf16[512,128]{1,0:T(8,128)(2,1)S(1)} %copy-done.6, ...), custom_call_target="tpu_custom_call" | custom-call | tf_op jit(solution)/shard_map/extend_add/pallas_call | solution.py:225
  137.3 0.0 copy-start.3
  137.3 1.0 copy-done.3
  138.3 0.0 copy-start.4
  138.3 1.0 copy-done.4
  139.3 0.0 copy-start.5
  139.3 0.7 copy-done.5
  140.0 73.3 %sketch_gather.1 = (bf16[8,128,1280]{2,1,0:T(8,128)(2,1)}, bf16[16,5,256,128]{3,2,1,0:T(8,128)(2,1)}, bf16[8,5,32,1280]{3,2,1,0:T(8,128)(2,1)}) custom-call(bf16[1024,512]{1,0:T(8,128)(2,1)} %copy-done.3, bf16[256,2048]{1,0:T(8,128)(2,1)} %copy-done.4, bf16[256,512]{1,0:T(8,128)(2,1)} %copy-done.5), custom_call_target="tpu_custom_call" | custom-call | tf_op jit(solution)/shard_map/sketch_gather/pallas_call | solution.py:464
  213.3 39.0 %panel_update.1 = bf16[1024,2048]{1,0:T(8,128)(2,1)} custom-call(bf16[1024,1280]{1,0:T(8,128)(2,1)} %bitcast.9, bf16[16,5,256,128]{3,2,1,0:T(8,128)(2,1)} %get-tuple-element.20.sall_ref, bf16[8,5,32,1280]{3,2,1,0:T(8,128)(2,1)} %get-tuple-element.21.tall_ref, bf16[128,128]{1,0:T(8,128)(2,1)} %core_ref.1, f32[1024,2048]{1,0:T(8,128)} %get-tuple-element.22.grid_ref), custom_call_target="tpu_custom_call" | custom-call | tf_op jit(solution)/shard_map/panel_update/pallas_call | solution.py:593
  (4 shorter events, 0.1 us)
Async XLA Ops:
  3.2 121.5 %copy-start.1 = (bf16[1024,2048]{1,0:T(8,128)(2,1)S(1)}, bf16[1024,2048]{1,0:T(8,128)(2,1)}, u32[]{:S(2)}) copy-start(bf16[1024,2048]{1,0:T(8,128)(2,1)} %front_ref.1) | copy-start | bytes 12582916
  3.3 2.3 copy-start.2
  5.6 119.1 %copy-start.6 = (bf16[512,128]{1,0:T(8,128)(2,1)S(1)}, bf16[512,128]{1,0:T(8,128)(2,1)}, u32[]{:S(2)}) copy-start(bf16[512,128]{1,0:T(8,128)(2,1)} %omega_ref.1) | copy-start | bytes 393220
  121.4 3.2 %copy-start = (bf16[128,2,128,128]{3,2,1,0:T(8,128)(2,1)}, bf16[128,2,128,128]{3,2,1,0:T(8,128)(2,1)S(1)}, u32[]{:S(2)}) copy-start(bf16[128,2,128,128]{3,2,1,0:T(8,128)(2,1)S(1)} %get-tuple-element.15.got_ref) | copy-start | bytes 25165828
  124.7 0.9 copy-start.7
  137.3 1.0 copy-start.3
  138.3 1.0 copy-start.4
  139.3 0.7 copy-start.5

commit v2 on v1

v2 whole, which is shorter than its diff:
```python
import functools

import jax
import jax.numpy as jnp
from jax import lax
from jax.experimental import pallas as pl
from jax.experimental.pallas import tpu as pltpu
from jax.sharding import PartitionSpec as P

PB = 512
SK = 128
TILE = 128
PANELS = 10
CAP = 2
ND = 128
NR = 16
NC = 8
ROWS = 1024
COLS = 2048
RANK = PANELS * SK
RSRC = 5
CSRC = 3
MESH = pl.DeviceIdType.MESH
MIB = 2**20


def div(a, b):
    return lax.div(a, jnp.int32(b))


def rem(a, b):
    return lax.rem(a, jnp.int32(b))


def partner(me, step):
    j = rem(step * 31, 128)
    bit = lambda p: rem(div(j, 2**p), 2)
    dx = bit(5) * 2 + bit(2)
    dz = bit(0) * 2 + bit(1)
    dy = bit(6) * 2 + bit(4)
    dk = bit(3)
    x = rem(div(me, 32) + dx, 4)
    z = rem(div(me, 8) + dz, 4)
    y = rem(div(me, 2) + dy, 4)
    k = rem(me + dk, 2)
    return x * 32 + z * 8 + y * 2 + k


def exchange_kernel(
    idx_ref, slot_ref, tiles_ref, got_ref, gslot_ref, send, lsem, ssem, rsem, slot_ssem, slot_rsem
):
    me = lax.axis_index("row") * NC + lax.axis_index("col")
    barrier = pltpu.get_barrier_semaphore()

    def greet(step, carry):
        p = partner(me, step)
        pl.semaphore_signal(barrier, inc=1, device_id=(div(p, NC), rem(p, NC)), device_id_type=MESH)
        return carry

    lax.fori_loop(1, ND, greet, 0)
    own_slot = pltpu.make_async_copy(slot_ref.at[me], gslot_ref.at[me], lsem.at[0])
    own_slot.start()

    def pack(p):
        for k in range(CAP):
            send[p, k] = tiles_ref[idx_ref[k, p]]

    pack(me)
    own = pltpu.make_async_copy(send.at[me], got_ref.at[me], lsem.at[1])
    own.start()
    pl.semaphore_wait(barrier, ND - 1)

    def copies(p, landing):
        device = (div(p, NC), rem(p, NC))
        tile = pltpu.make_async_remote_copy(
            src_ref=send.at[p], dst_ref=got_ref.at[landing], send_sem=ssem.at[p], recv_sem=rsem.at[landing],
            device_id=device, device_id_type=MESH,
        )
        slot = pltpu.make_async_remote_copy(
            src_ref=slot_ref.at[p], dst_ref=gslot_ref.at[landing], send_sem=slot_ssem.at[p],
            recv_sem=slot_rsem.at[landing], device_id=device, device_id_type=MESH,
        )
        return tile, slot

    def post(step, carry):
        p = partner(me, step)
        pack(p)
        tile, slot = copies(p, me)
        tile.start()
        slot.start()
        return carry

    lax.fori_loop(1, ND, post, 0)

    def finish(step, carry):
        p = partner(me, step)
        tile, slot = copies(p, p)
        tile.wait()
        slot.wait()
        return carry

    lax.fori_loop(1, ND, finish, 0)
    own_slot.wait()
    own.wait()


def exchange(idx, slots, tiles):
    vmem = pl.BlockSpec(memory_space=pltpu.VMEM)
    return pl.pallas_call(
        exchange_kernel,
        out_shape=(
            jax.ShapeDtypeStruct((ND, CAP, TILE, TILE), jnp.bfloat16),
            jax.ShapeDtypeStruct((ND, 1, TILE), jnp.int32),
        ),
        in_specs=[pl.BlockSpec(memory_space=pltpu.SMEM), vmem, vmem],
        out_specs=(vmem, vmem),
        scratch_shapes=[
            pltpu.VMEM((ND, CAP, TILE, TILE), jnp.bfloat16),
            pltpu.SemaphoreType.DMA((2,)),
            pltpu.SemaphoreType.DMA((ND,)),
            pltpu.SemaphoreType.DMA((ND,)),
            pltpu.SemaphoreType.DMA((ND,)),
            pltpu.SemaphoreType.DMA((ND,)),
        ],
        compiler_params=pltpu.CompilerParams(
            collective_id=0, has_side_effects=True, vmem_limit_bytes=12 * MIB
        ),
        name="tile_exchange",
    )(idx, slots, tiles)


def assemble_kernel(slot_ref, front_ref, got_ref, omega_ref, psi_ref, grid, b_ref, s_ref, t_ref):
    r = lax.axis_index("row")
    c = lax.axis_index("col")

    def widen(i, carry):
        rows = pl.ds(pl.multiple_of(i * 64, 64), 64)
        grid[rows, :] = front_ref[rows, :].astype(jnp.float32)
        return carry

    lax.fori_loop(0, ROWS // 64, widen, 0)

    def add(source, carry):
        for k in range(CAP):
            slot = slot_ref[source, k]

            @pl.when(slot >= 0)
            def _():
                rows = pl.ds(pl.multiple_of(div(slot, COLS // TILE) * TILE, TILE), TILE)
                cols = pl.ds(pl.multiple_of(rem(slot, COLS // TILE) * TILE, TILE), TILE)
                grid[rows, cols] += got_ref[source, k].astype(jnp.float32)

        return carry

    lax.fori_loop(0, ND, add, 0)

    @pl.when(c < CSRC)
    def _():
        def rows_of(i, carry):
            rows = pl.ds(pl.multiple_of(i * 256, 256), 256)
            for k in range(4):
                block = grid[rows, k * PB : (k + 1) * PB].astype(jnp.bfloat16)
                b_ref[rows, k * SK : (k + 1) * SK] = jnp.dot(
                    block, omega_ref[...], preferred_element_type=jnp.float32
                ).astype(jnp.bfloat16)
            return carry

        lax.fori_loop(0, ROWS // 256, rows_of, 0)

    @pl.when(r < RSRC)
    def _():
        psi_t = psi_ref[...].T
        for j in range(2):
            def cols_of(i, carry):
                cols = pl.ds(pl.multiple_of(i * 512, 512), 512)
                block = grid[j * PB : (j + 1) * PB, cols].astype(jnp.bfloat16)
                s_ref[j * SK : (j + 1) * SK, cols] = jnp.dot(
                    psi_t, block, preferred_element_type=jnp.float32
                ).astype(jnp.bfloat16)
                return carry

            lax.fori_loop(0, COLS // 512, cols_of, 0)

        @pl.when(c < CSRC)
        def _():
            for j in range(2):
                t_ref[j * SK : (j + 1) * SK, :] = jnp.dot(
                    psi_t, b_ref[j * PB : (j + 1) * PB, :], preferred_element_type=jnp.float32
                ).astype(jnp.bfloat16)


def assemble(slots, front, got, omega, psi):
    vmem = pl.BlockSpec(memory_space=pltpu.VMEM)
    return pl.pallas_call(
        assemble_kernel,
        out_shape=(
            jax.ShapeDtypeStruct((ROWS, COLS), jnp.float32),
            jax.ShapeDtypeStruct((ROWS, 4 * SK), jnp.bfloat16),
            jax.ShapeDtypeStruct((2 * SK, COLS), jnp.bfloat16),
            jax.ShapeDtypeStruct((2 * SK, 4 * SK), jnp.bfloat16),
        ),
        in_specs=[pl.BlockSpec(memory_space=pltpu.SMEM), vmem, vmem, vmem, vmem],
        out_specs=(vmem, vmem, vmem, vmem),
        compiler_params=pltpu.CompilerParams(vmem_limit_bytes=4 * MIB),
        name="extend_add",
    )(slots, front, got, omega, psi)


TR = 2 * SK // NC
WIDE = 4 * TILE
BLOCKS = COLS // WIDE
STEPS = (1, 3, 2)


def eliminate(tall, core, state, lmat, rmat):
    f32 = jnp.float32
    bf16 = jnp.bfloat16
    for cc in range(NC):
        for q in range(RSRC):
            lo = q * 2 * SK + cc * TR
            state[lo : lo + TR, :] = tall[cc, q].astype(f32)
    row = lax.broadcasted_iota(jnp.int32, (SK, SK), 0)
    col = lax.broadcasted_iota(jnp.int32, (SK, SK), 1)
    eye = jnp.where(row == col, 1.0, 0.0).astype(bf16)
    for s in range(PANELS):
        lo, hi = s * SK, (s + 1) * SK
        if s % 2 == 0:
            lmat[hi : hi + SK, lo:hi] = jnp.zeros((SK, SK), bf16)
            rmat[lo:hi, hi : hi + SK] = jnp.zeros((SK, SK), bf16)
        lmat[lo:hi, lo:hi] = core
        rmat[lo:hi, lo:hi] = eye
        if s:
            lmat[:lo, lo:hi] = jnp.dot(state[:lo, lo:hi].astype(bf16), core, preferred_element_type=f32).astype(bf16)
            rmat[lo:hi, :lo] = state[lo:hi, :lo].astype(bf16)
        if s == PANELS - 1:
            break
        below = jnp.dot(state[hi:, lo:hi].astype(bf16), core, preferred_element_type=f32).astype(bf16)
        beside = state[lo:hi, hi:].astype(bf16)
        state[hi:, hi:] -= jnp.dot(below, beside, preferred_element_type=f32)
        state[lo:hi, hi:] = -jnp.dot(core, beside, preferred_element_type=f32)
        state[hi:, lo:hi] = -below.astype(f32)
        if s:
            state[:lo, hi:] -= jnp.dot(lmat[:lo, lo:hi], beside, preferred_element_type=f32)
            state[hi:, :lo] -= jnp.dot(below, rmat[lo:hi, :lo], preferred_element_type=f32)


def factor_kernel(
    b_ref, s_ref, t_ref, core_ref, left, right,
    ball, sall, tall, state, lmat, rmat,
    lsem, t1s, t1r, t2s, t2r, t3s, t3r, bss, bsr, bas, bar, sss, ssr, s2s, s2r, s3s, s3r,
):
    r = lax.axis_index("row")
    c = lax.axis_index("col")
    x, z = div(r, 4), rem(r, 4)
    y, k = div(c, 2), rem(c, 2)
    other = y * 2 + (1 - k)
    f32 = jnp.float32
    bf16 = jnp.bfloat16

    barrier = pltpu.get_barrier_semaphore()
    for i in range(1, NR):
        pl.semaphore_signal(barrier, inc=1, device_id=(rem(r + i, NR), c), device_id_type=MESH)
    for i in range(1, NC):
        pl.semaphore_signal(barrier, inc=1, device_id=(r, rem(c + i, NC)), device_id_type=MESH)
    pl.semaphore_wait(barrier, NR - 1 + NC - 1)

    def remote(src, dst, send, recv, device):
        return pltpu.make_async_remote_copy(
            src_ref=src, dst_ref=dst, send_sem=send, recv_sem=recv, device_id=device, device_id_type=MESH
        )

    widths = [4 * SK, 4 * SK, 2 * SK]

    def t1(cc, src_c, sem):
        w = widths[src_c]
        return remote(
            t_ref.at[pl.ds(pl.multiple_of(cc * TR, TR), TR), pl.ds(0, w)],
            tall.at[cc, r, :, pl.ds(src_c * 4 * SK, w)],
            t1s.at[sem], t1r.at[src_c], (r, cc),
        )

    def b1(cc, src_c, sem):
        w = widths[src_c]
        return remote(
            b_ref.at[pl.ds(pl.multiple_of(cc * TILE, TILE), TILE), pl.ds(0, w)],
            ball.at[cc, :, pl.ds(src_c * 4 * SK, w)],
            bss.at[sem], bsr.at[src_c], (r, cc),
        )

    def s1(half, rr, src_r, sem):
        rows = pl.ds(half * SK, SK)
        return remote(
            s_ref.at[rows, pl.ds(pl.multiple_of(rr * TILE, TILE), TILE)], sall.at[rr, src_r, rows, :],
            sss.at[half, sem], ssr.at[half, src_r], (rr, c),
        )

    def own_t(src_c):
        w = widths[src_c]
        return pltpu.make_async_copy(
            t_ref.at[pl.ds(pl.multiple_of(c * TR, TR), TR), pl.ds(0, w)],
            tall.at[c, r, :, pl.ds(src_c * 4 * SK, w)], lsem.at[0],
        )

    def own_b(src_c):
        w = widths[src_c]
        return pltpu.make_async_copy(
            b_ref.at[pl.ds(pl.multiple_of(c * TILE, TILE), TILE), pl.ds(0, w)],
            ball.at[c, :, pl.ds(src_c * 4 * SK, w)], lsem.at[1],
        )

    def own_s():
        return pltpu.make_async_copy(
            s_ref.at[:, pl.ds(pl.multiple_of(r * TILE, TILE), TILE)], sall.at[r, r], lsem.at[2]
        )

    @pl.when(r < RSRC)
    def _():
        for src_c in range(CSRC):
            @pl.when(c == src_c)
            def _():
                own_t(src_c).start()
                for i in range(1, NC):
                    t1(rem(c + i, NC), src_c, i).start()

    for src_c in range(CSRC):
        @pl.when(c == src_c)
        def _():
            own_b(src_c).start()
            for i in range(1, NC):
                b1(rem(c + i, NC), src_c, i).start()

    homes = [(0, 0), (0, 1), (0, 2), (0, 3), (1, 0)]

    def t2(src_r, rr, sem):
        return remote(tall.at[c, src_r], tall.at[c, src_r], t2s.at[src_r, sem], t2r.at[src_r], (rr, c))

    @pl.when(r < RSRC)
    def _():
        for src_c in range(CSRC):
            @pl.when(c != src_c)
            def _():
                t1(c, src_c, 0).wait_recv()

            @pl.when(c == src_c)
            def _():
                own_t(src_c).wait()

    for src_r, (hx, hz) in enumerate(homes):
        @pl.when(r == src_r)
        def _():
            for n, d in enumerate(STEPS):
                t2(src_r, rem(x + d, 4) * 4 + z, n).start()
            for n, d in enumerate(STEPS):
                t2(src_r, x * 4 + rem(z + d, 4), 3 + n).start()

    axes = (("x", "z"), ("z", "x"))

    @pl.when(r < RSRC)
    def _():
        own_s().start()
        for half in range(2):
            for i in range(1, NR):
                s1(half, rem(r + i, NR), r, i).start()

    for src_r, (hx, hz) in enumerate(homes):
        @pl.when((z == hz) & (x != hx))
        def _():
            t2(src_r, r, 0).wait_recv()
            for n, d in enumerate(STEPS):
                t2(src_r, x * 4 + rem(z + d, 4), 3 + n).start()

    up = rem(y + 1, 4) * 2 + k
    down = rem(y + 3, 4) * 2 + k
    far = rem(y + 2, 4) * 2 + k

    def t3(piece, h, cc, sem):
        part = tall.at[piece, :, pl.ds(h * (TR // 2), TR // 2), :]
        return remote(part, part, t3s.at[sem], t3r.at[piece, h], (r, cc))

    def b3(piece, h, cc, sem):
        part = ball.at[piece, pl.ds(h * (TILE // 2), TILE // 2), :]
        return remote(part, part, bas.at[sem], bar.at[piece, h], (r, cc))

    def post_own(copy):
        copy(c, 0, up, 0).start()
        copy(c, 1, down, 1).start()
        copy(c, 1, up, 2).start()
        copy(c, 0, down, 3).start()
        copy(c, 0, other, 4).start()
        copy(c, 1, other, 5).start()

    def post_relays(copy):
        copy(down, 0, c, 0).wait_recv()
        copy(down, 0, up, 6).start()
        copy(down, 0, other, 7).start()
        copy(up, 1, c, 0).wait_recv()
        copy(up, 1, down, 8).start()
        copy(up, 1, other, 9).start()
        copy(down, 1, c, 0).wait_recv()
        copy(down, 1, other, 10).start()
        copy(up, 0, c, 0).wait_recv()
        copy(up, 0, other, 11).start()

    def post_far(copy):
        for h in range(2):
            copy(far, h, c, 0).wait_recv()
            copy(far, h, other, 12 + h).start()

    def wait_other(copy):
        for yy in range(4):
            for h in range(2):
                copy(yy * 2 + (1 - k), h, c, 0).wait_recv()

    for src_c in range(CSRC):
        @pl.when(c != src_c)
        def _():
            b1(c, src_c, 0).wait_recv()

        @pl.when(c == src_c)
        def _():
            own_b(src_c).wait()
    post_own(b3)

    for src_r, (hx, hz) in enumerate(homes):
        @pl.when(z != hz)
        def _():
            t2(src_r, r, 0).wait_recv()
    post_own(t3)

    def along(axis, d):
        if axis == "x":
            return rem(x + d, 4) * 4 + z
        return x * 4 + rem(z + d, 4)

    def first(half, piece, rr, sem):
        part = sall.at[piece, :, pl.ds(half * SK, SK), :]
        return remote(part, part, s2s.at[half, sem], s2r.at[half, piece], (rr, c))

    def second(half, piece, q, rr, sem):
        part = sall.at[piece, :, pl.ds(half * SK + q * (SK // 2), SK // 2), :]
        return remote(part, part, s3s.at[half, sem], s3r.at[half, piece, q], (rr, c))

    def post_second(half, piece, m):
        plus = along(axes[half][1], 1)
        minus = along(axes[half][1], 3)
        second(half, piece, 0, plus, 6 * m).start()
        second(half, piece, 1, minus, 6 * m + 1).start()
        second(half, piece, 1, plus, 6 * m + 2).start()
        second(half, piece, 0, minus, 6 * m + 3).start()

    def relay_second(half, d, m):
        for q, side, onward in ((0, 3, 1), (1, 1, 3)):
            if axes[half][0] == "x":
                piece = rem(x + d, 4) * 4 + rem(z + side, 4)
            else:
                piece = rem(x + side, 4) * 4 + rem(z + d, 4)
            second(half, piece, q, r, 0).wait_recv()
            second(half, piece, q, along(axes[half][1], onward), 6 * m + 4 + q).start()

    def settle(half, piece, distance):
        @pl.when(distance != 3)
        def _():
            second(half, piece, 0, r, 0).wait_recv()

        @pl.when(distance != 1)
        def _():
            second(half, piece, 1, r, 0).wait_recv()

    for half in range(2):
        for src_r in range(RSRC):
            @pl.when(r != src_r)
            def _():
                s1(half, r, src_r, 0).wait_recv()

            if half == 0:
                @pl.when(r == src_r)
                def _():
                    own_s().wait()
        for n, d in enumerate(STEPS):
            first(half, r, along(axes[half][0], d), n).start()
        post_second(half, r, 0)

    post_relays(b3)
    for half in range(2):
        relay_second(half, 0, 0)
    for m, d in enumerate(STEPS):
        for half in range(2):
            piece = along(axes[half][0], d)
            first(half, piece, r, 0).wait_recv()
            post_second(half, piece, 1 + m)
    post_relays(t3)
    post_far(b3)
    for half in range(2):
        relay_second(half, STEPS[0], 1)
    post_far(t3)
    for m in (1, 2):
        for half in range(2):
            relay_second(half, STEPS[m], 1 + m)
    wait_other(t3)

    core = core_ref[...]
    eliminate(tall, core, state, lmat, rmat)

    def right_block(i, carry):
        xx = rem(x + i, 4)
        for zz in range(4):
            piece = xx * 4 + zz
            dz = rem(zz - z + 4, 4)

            @pl.when(dz != 0)
            def _():
                settle(0, piece, dz)

            @pl.when(i != 0)
            def _():
                settle(1, piece, i)

        block = jnp.concatenate([sall[xx * 4 + h].reshape(RANK, TILE) for h in range(4)], axis=1)
        panel = c * (COLS // PB) + xx
        for q in range(RSRC):
            lo, hi = q * 2 * SK, (q + 1) * 2 * SK
            out = jnp.dot(rmat[lo:hi, :hi], block[:hi], preferred_element_type=f32)
            for j in range(2):
                part = out[j * SK : (j + 1) * SK]
                part = jnp.where(2 * q + j < panel, part, jnp.zeros_like(part))
                right[xx, lo + j * SK : lo + (j + 1) * SK, :] = part.astype(bf16)
        return carry

    lax.fori_loop(0, BLOCKS, right_block, 0)

    wait_other(b3)

    def left_rows(i, carry):
        panel = r * (ROWS // PB) + i
        block = jnp.concatenate([ball[i * 4 + h] for h in range(4)], axis=0)
        for q in range(RSRC):
            lo, hi = q * 2 * SK, (q + 1) * 2 * SK
            out = jnp.dot(block[:, :hi], lmat[:hi, lo:hi], preferred_element_type=f32)
            for j in range(2):
                part = out[:, j * SK : (j + 1) * SK]
                part = jnp.where(2 * q + j < panel, part, jnp.zeros_like(part))
                left[pl.ds(pl.multiple_of(i * PB, PB), PB), lo + j * SK : lo + (j + 1) * SK] = part.astype(bf16)
        return carry

    lax.fori_loop(0, ROWS // PB, left_rows, 0)

    @pl.when(r < RSRC)
    def _():
        for src_c in range(CSRC):
            @pl.when(c == src_c)
            def _():
                for i in range(1, NC):
                    t1(rem(c + i, NC), src_c, i).wait_send()
        for i in range(1, NR):
            for half in range(2):
                s1(half, rem(r + i, NR), r, i).wait_send()

    for src_c in range(CSRC):
        @pl.when(c == src_c)
        def _():
            for i in range(1, NC):
                b1(rem(c + i, NC), src_c, i).wait_send()
    for src_r, (hx, hz) in enumerate(homes):
        @pl.when(r == src_r)
        def _():
            for n in range(3):
                t2(src_r, rem(r + 1, NR), n).wait_send()

        @pl.when(z == hz)
        def _():
            for n in range(3):
                t2(src_r, rem(r + 1, NR), 3 + n).wait_send()
    for i in range(14):
        t3(c, 0, other, i).wait_send()
        b3(c, 0, other, i).wait_send()
    for half in range(2):
        for i in range(3):
            first(half, r, rem(r + 1, NR), i).wait_send()
        for i in range(24):
            second(half, r, 0, rem(r + 1, NR), i).wait_send()


def factors(b, s, t, core):
    vmem = pl.BlockSpec(memory_space=pltpu.VMEM)
    dma = pltpu.SemaphoreType.DMA
    bf16 = jnp.bfloat16
    return pl.pallas_call(
        factor_kernel,
        out_shape=(
            jax.ShapeDtypeStruct((ROWS, RANK), bf16),
            jax.ShapeDtypeStruct((BLOCKS, RANK, WIDE), bf16),
        ),
        in_specs=[vmem] * 4,
        out_specs=(vmem, vmem),
        scratch_shapes=[
            pltpu.VMEM((NC, TILE, RANK), bf16),
            pltpu.VMEM((NR, RSRC, 2 * SK, TILE), bf16),
            pltpu.VMEM((NC, RSRC, TR, RANK), bf16),
            pltpu.VMEM((RANK, RANK), jnp.float32),
            pltpu.VMEM((RANK, RANK), bf16),
            pltpu.VMEM((RANK, RANK), bf16),
            dma((3,)),
            dma((NC,)), dma((CSRC,)), dma((RSRC, 6)), dma((RSRC,)), dma((14,)), dma((NC, 2)),
            dma((NC,)), dma((CSRC,)), dma((14,)), dma((NC, 2)),
            dma((2, NR)), dma((2, RSRC)), dma((2, 3)), dma((2, NR)), dma((2, 24)), dma((2, NR, 2)),
        ],
        compiler_params=pltpu.CompilerParams(
            collective_id=1, has_side_effects=True, vmem_limit_bytes=28 * MIB
        ),
        name="panel_factors",
    )(b, s, t, core)


UR = 512


def update_kernel(left, right, grid, out_ref, obuf, osem):
    f32 = jnp.float32
    n = ROWS // UR

    def of_rows(i):
        return pl.ds(pl.multiple_of(i * UR, UR), UR)

    def store(i):
        return pltpu.make_async_copy(obuf.at[i], out_ref.at[of_rows(i)], osem.at[i])

    def rows(i, carry):
        def block(q, carry):
            cols = pl.ds(pl.multiple_of(q * WIDE, WIDE), WIDE)
            product = jnp.dot(left[of_rows(i), :], right[q], preferred_element_type=f32)
            obuf[i, :, cols] = (grid[of_rows(i), cols] - product).astype(jnp.bfloat16)
            return carry

        lax.fori_loop(0, BLOCKS, block, 0)
        store(i).start()
        return carry

    lax.fori_loop(0, n, rows, 0)
    for i in range(n):
        store(i).wait()


def update(left, right, grid):
    hbm = pl.BlockSpec(memory_space=pltpu.HBM)
    vmem = pl.BlockSpec(memory_space=pltpu.VMEM)
    n = ROWS // UR
    return pl.pallas_call(
        update_kernel,
        out_shape=jax.ShapeDtypeStruct((ROWS, COLS), jnp.bfloat16),
        in_specs=[vmem, vmem, vmem],
        out_specs=hbm,
        scratch_shapes=[pltpu.VMEM((n, UR, COLS), jnp.bfloat16), pltpu.SemaphoreType.DMA((n,))],
        compiler_params=pltpu.CompilerParams(vmem_limit_bytes=10 * MIB),
        name="panel_update",
    )(left, right, grid)


def shards(front, tiles, counts, dest_owner, dest_slot, omega, psi, core):
    owners = dest_owner[:, 0]
    strip = jnp.arange(ND, dtype=jnp.int32)
    same = owners[:, None] == owners[None, :]
    before = strip[None, :] < strip[:, None]
    ranks = jnp.sum((same & before).astype(jnp.int32), axis=1)
    valid = strip < counts[0]
    named = strip[None, :, None] == owners[None, None, :]
    hit = named & (ranks[None, None, :] == jnp.arange(CAP, dtype=jnp.int32)[:, None, None])
    idx = jnp.sum(jnp.where(hit, strip[None, None, :], 0), axis=2)
    slots = jnp.sum(jnp.where(hit & valid[None, None, :], dest_slot[None, None, :] + 1, 0), axis=2) - 1
    slots = jnp.pad(slots.T[:, None, :], ((0, 0), (0, 0), (0, TILE - CAP)))
    got, got_slots = exchange(idx, slots, tiles)
    grid, b, s, t = assemble(got_slots[:, 0, :], front, got, omega, psi)
    left, right = factors(b, s, t, core)
    return update(left, right, grid)


def solution(mesh):
    in_specs = (
        P("row", "col"),
        P(("row", "col"), None, None),
        P(("row", "col")),
        P(("row", "col"), None),
        P(("row", "col")),
        P(),
        P(),
        P(),
    )
    out_specs = P("row", "col")
    return jax.shard_map(shards, mesh=mesh, in_specs=in_specs, out_specs=out_specs, check_vma=False)
```

time: 253 us -> 213 us (0.84)
  the two profiles are of different devices: /device:TPU:97 before, /device:TPU:80 now
where the time goes in v2:
time: 213 us; the launch traced here: 212 us
  Pallas kernels  206 us (97%)
  local copies, waits for them, and re-layouts  3.41 us (2%)
  other arithmetic  2.4 us (1%)
    pallas_call x1, Pallas kernels, exchange(): pl.pallas_call(exchange_kernel, out_shape=(jax.ShapeDtypeStruct((ND, CAP,...  117 us
    pallas_call x1, Pallas kernels, factors(): pl.pallas_call(factor_kernel, out_shape=(jax.ShapeDtypeStruct((ROWS, RANK...  72.2 us
    pallas_call x1, Pallas kernels, assemble(): pl.pallas_call(assemble_kernel, out_shape=(jax.ShapeDtypeStruct((ROWS, CO...  8.42 us
    pallas_call x1, Pallas kernels, update(): pl.pallas_call(update_kernel, out_shape=jax.ShapeDtypeStruct((ROWS, COLS)...  8.09 us

profile of v2, /device:TPU:80, one launch (start us, length us, event | category | flops | bytes accessed | tf_op | source)
XLA Modules:
  0.0 212.4 jit_solution(4315451749671036528)
XLA Ops:
  0.7 0.9 convert_reduce_fusion
  1.6 0.7 broadcast_add_fusion.1
  2.2 0.7 iota_compare_fusion.1
  2.9 0.2 select_reduce_fusion
  3.1 0.1 copy.11
  3.2 0.0 copy-start
  3.3 0.0 copy-start.1
  3.3 2.3 %copy-done.1 = bf16[128,128,128]{2,1,0:T(8,128)(2,1)S(1)} copy-done((bf16[128,128,128]{2,1,0:T(8,128)(2,1)S(1)}, bf16[128,128,128]{2,1,0:T(8,128)(2,1)}, u32[]{:S(2)}) %copy-start.1) | copy-done | bytes 4194328
  5.6 0.0 copy-start.2
  5.6 116.9 %tile_exchange.1 = (bf16[128,2,128,128]{3,2,1,0:T(8,128)(2,1)S(1)}, s32[128,1,128]{2,1,0:T(1,128)S(1)}) custom-call(s32[2,128]{1,0:T(2,128)S(1)} %get-tuple-element.22.idx_ref, s32[128,1,128]{2,1,0:T(1,128)S(1)} %pad.4.slot_ref, bf16[128,128,128]{2,1,0:T(8,128)(2,1)S(1)} %copy-done.1), custom_call_target="tpu_custom_call" | custom-call | tf_op jit(solution)/shard_map/tile_exchange/pallas_call | solution.py:109
  122.5 0.0 copy-done
  122.5 0.0 copy-done.2
  122.5 0.0 copy-start.3
  122.6 0.9 copy-done.3
  123.4 0.0 copy-start.4
  123.4 8.4 %extend_add.1 = (f32[1024,2048]{1,0:T(8,128)S(1)}, bf16[1024,512]{1,0:T(8,128)(2,1)S(1)}, bf16[256,2048]{1,0:T(8,128)(2,1)S(1)}, bf16[256,512]{1,0:T(8,128)(2,1)S(1)}) custom-call(s32[128,128]{1,0:T(8,128)S(1)} %bitcast.7, bf16[1024,2048]{1,0:T(8,128)(2,1)S(1)} %copy-done, bf16[128,2,128,128]{3,2,1,0:T(8,128)(2,1)S(1)} %get-tuple-element.14.got_ref, ...), custom_call_target="tpu_custom_call" | custom-call | tf_op jit(solution)/shard_map/extend_add/pallas_call | solution.py:194
  131.9 0.0 copy-done.4
  131.9 72.2 %panel_factors.1 = (bf16[1024,1280]{1,0:T(8,128)(2,1)S(1)}, bf16[4,1280,512]{2,1,0:T(8,128)(2,1)S(1)}) custom-call(bf16[1024,512]{1,0:T(8,128)(2,1)S(1)} %get-tuple-element.15.b_ref, bf16[256,2048]{1,0:T(8,128)(2,1)S(1)} %get-tuple-element.16.s_ref, bf16[256,512]{1,0:T(8,128)(2,1)S(1)} %get-tuple-element.17.t_ref, bf16[128,128]{1,0:T(8,128)(2,1)S(1)} %copy-done.4), custom_call_target="tpu_custom_call" | custom-call | tf_op jit(solution)/shard_map/panel_factors/pallas_call | solution.py:587
  204.1 8.1 %panel_update.1 = bf16[1024,2048]{1,0:T(8,128)(2,1)} custom-call(bf16[1024,1280]{1,0:T(8,128)(2,1)S(1)} %get-tuple-element.18.left, bf16[4,1280,512]{2,1,0:T(8,128)(2,1)S(1)} %get-tuple-element.19.right, f32[1024,2048]{1,0:T(8,128)S(1)} %get-tuple-element.20.grid), custom_call_target="tpu_custom_call" | custom-call | tf_op jit(solution)/shard_map/panel_update/pallas_call | solution.py:647
  (4 shorter events, 0.1 us)
Async XLA Ops:
  3.2 119.3 %copy-start = (bf16[1024,2048]{1,0:T(8,128)(2,1)S(1)}, bf16[1024,2048]{1,0:T(8,128)(2,1)}, u32[]{:S(2)}) copy-start(bf16[1024,2048]{1,0:T(8,128)(2,1)} %front_ref.1) | copy-start | bytes 12582916
  3.3 2.3 %copy-start.1 = (bf16[128,128,128]{2,1,0:T(8,128)(2,1)S(1)}, bf16[128,128,128]{2,1,0:T(8,128)(2,1)}, u32[]{:S(2)}) copy-start(bf16[128,128,128]{2,1,0:T(8,128)(2,1)} %tiles_ref.1) | copy-start | bytes 12582916
  5.6 116.9 %copy-start.2 = (bf16[512,128]{1,0:T(8,128)(2,1)S(1)}, bf16[512,128]{1,0:T(8,128)(2,1)}, u32[]{:S(2)}) copy-start(bf16[512,128]{1,0:T(8,128)(2,1)} %omega_ref.1) | copy-start | bytes 393220
  122.5 0.9 copy-start.3
  123.4 8.4 %copy-start.4 = (bf16[128,128]{1,0:T(8,128)(2,1)S(1)}, bf16[128,128]{1,0:T(8,128)(2,1)}, u32[]{:S(2)}) copy-start(bf16[128,128]{1,0:T(8,128)(2,1)} %core_ref.1) | copy-start | bytes 98308

commit v3 on v2

--- a/solution.py
+++ b/solution.py
@@ -35,10 +35,10 @@
 def partner(me, step):
     j = rem(step * 31, 128)
     bit = lambda p: rem(div(j, 2**p), 2)
-    dx = bit(5) * 2 + bit(2)
-    dz = bit(0) * 2 + bit(1)
-    dy = bit(6) * 2 + bit(4)
-    dk = bit(3)
+    dx = bit(0) * 2 + bit(3)
+    dz = bit(5) * 2 + bit(4)
+    dy = bit(6) * 2 + bit(2)
+    dk = bit(1)
     x = rem(div(me, 32) + dx, 4)
     z = rem(div(me, 8) + dz, 4)
     y = rem(div(me, 2) + dy, 4)
@@ -123,7 +123,7 @@
             pltpu.SemaphoreType.DMA((ND,)),
         ],
         compiler_params=pltpu.CompilerParams(
-            collective_id=0, has_side_effects=True, vmem_limit_bytes=12 * MIB
+            collective_id=0, has_side_effects=True, vmem_limit_bytes=14 * MIB
         ),
         name="tile_exchange",
     )(idx, slots, tiles)
@@ -201,7 +201,7 @@
         ),
         in_specs=[pl.BlockSpec(memory_space=pltpu.SMEM), vmem, vmem, vmem, vmem],
         out_specs=(vmem, vmem, vmem, vmem),
-        compiler_params=pltpu.CompilerParams(vmem_limit_bytes=4 * MIB),
+        compiler_params=pltpu.CompilerParams(vmem_limit_bytes=6 * MIB),
         name="extend_add",
     )(slots, front, got, omega, psi)
 
@@ -210,9 +210,14 @@
 WIDE = 4 * TILE
 BLOCKS = COLS // WIDE
 STEPS = (1, 3, 2)
-
-
-def eliminate(tall, core, state, lmat, rmat):
+PLANE = (
+    (1, 0), (3, 0), (0, 1), (2, 0), (1, 1), (3, 1), (0, 3), (2, 1),
+    (1, 3), (3, 3), (0, 2), (2, 3), (1, 2), (3, 2), (2, 2),
+)
+LINE = ((1, 0), (3, 0), (1, 1), (3, 1), (2, 0), (2, 1), (0, 1))
+
+
+def eliminate(tall, core, state, lmat, rmat, between):
     f32 = jnp.float32
     bf16 = jnp.bfloat16
     for cc in range(NC):
@@ -224,6 +229,8 @@
     eye = jnp.where(row == col, 1.0, 0.0).astype(bf16)
     for s in range(PANELS):
         lo, hi = s * SK, (s + 1) * SK
+        if s in between:
+            between[s]()
         if s % 2 == 0:
             lmat[hi : hi + SK, lo:hi] = jnp.zeros((SK, SK), bf16)
             rmat[lo:hi, hi : hi + SK] = jnp.zeros((SK, SK), bf16)
@@ -319,15 +326,15 @@
             @pl.when(c == src_c)
             def _():
                 own_t(src_c).start()
-                for i in range(1, NC):
-                    t1(rem(c + i, NC), src_c, i).start()
+                for i, (dy, dk) in enumerate(LINE):
+                    t1(rem(y + dy, 4) * 2 + rem(k + dk, 2), src_c, 1 + i).start()
 
     for src_c in range(CSRC):
         @pl.when(c == src_c)
         def _():
             own_b(src_c).start()
-            for i in range(1, NC):
-                b1(rem(c + i, NC), src_c, i).start()
+            for i, (dy, dk) in enumerate(LINE):
+                b1(rem(y + dy, 4) * 2 + rem(k + dk, 2), src_c, 1 + i).start()
 
     homes = [(0, 0), (0, 1), (0, 2), (0, 3), (1, 0)]
 
@@ -350,7 +357,6 @@
         def _():
             for n, d in enumerate(STEPS):
                 t2(src_r, rem(x + d, 4) * 4 + z, n).start()
-            for n, d in enumerate(STEPS):
                 t2(src_r, x * 4 + rem(z + d, 4), 3 + n).start()
 
     axes = (("x", "z"), ("z", "x"))
@@ -359,15 +365,22 @@
     def _():
         own_s().start()
         for half in range(2):
-            for i in range(1, NR):
-                s1(half, rem(r + i, NR), r, i).start()
+            for i, (dx, dz) in enumerate(PLANE):
+                s1(half, rem(x + dx, 4) * 4 + rem(z + dz, 4), r, 1 + i).start()
 
     for src_r, (hx, hz) in enumerate(homes):
-        @pl.when((z == hz) & (x != hx))
-        def _():
-            t2(src_r, r, 0).wait_recv()
-            for n, d in enumerate(STEPS):
-                t2(src_r, x * 4 + rem(z + d, 4), 3 + n).start()
+        if src_r < 4:
+            @pl.when((z == hz) & (x != hx))
+            def _():
+                t2(src_r, r, 0).wait_recv()
+                for n, d in enumerate(STEPS):
+                    t2(src_r, x * 4 + rem(z + d, 4), 3 + n).start()
+        else:
+            @pl.when((x == hx) & (z != hz))
+            def _():
+                t2(src_r, r, 0).wait_recv()
+                for n, d in enumerate(STEPS):
+                    t2(src_r, rem(x + d, 4) * 4 + z, n).start()
 
     up = rem(y + 1, 4) * 2 + k
     down = rem(y + 3, 4) * 2 + k
@@ -422,7 +435,7 @@
     post_own(b3)
 
     for src_r, (hx, hz) in enumerate(homes):
-        @pl.when(z != hz)
+        @pl.when((z != hz) if src_r < 4 else (x != hx))
         def _():
             t2(src_r, r, 0).wait_recv()
     post_own(t3)
@@ -493,13 +506,14 @@
     for half in range(2):
         relay_second(half, STEPS[0], 1)
     post_far(t3)
-    for m in (1, 2):
+    wait_other(t3)
+
+    def relay_both(m):
         for half in range(2):
             relay_second(half, STEPS[m], 1 + m)
-    wait_other(t3)
 
     core = core_ref[...]
-    eliminate(tall, core, state, lmat, rmat)
+    eliminate(tall, core, state, lmat, rmat, {1: lambda: relay_both(1), 5: lambda: relay_both(2)})
 
     def right_block(i, carry):
         xx = rem(x + i, 4)
@@ -561,15 +575,17 @@
             for i in range(1, NC):
                 b1(rem(c + i, NC), src_c, i).wait_send()
     for src_r, (hx, hz) in enumerate(homes):
+        leg = 0 if src_r < 4 else 3
+
         @pl.when(r == src_r)
         def _():
             for n in range(3):
-                t2(src_r, rem(r + 1, NR), n).wait_send()
-
-        @pl.when(z == hz)
+                t2(src_r, rem(r + 1, NR), leg + n).wait_send()
+
+        @pl.when((z == hz) if src_r < 4 else (x == hx))
         def _():
             for n in range(3):
-                t2(src_r, rem(r + 1, NR), 3 + n).wait_send()
+                t2(src_r, rem(r + 1, NR), 3 - leg + n).wait_send()
     for i in range(14):
         t3(c, 0, other, i).wait_send()
         b3(c, 0, other, i).wait_send()
@@ -605,7 +621,7 @@
             dma((2, NR)), dma((2, RSRC)), dma((2, 3)), dma((2, NR)), dma((2, 24)), dma((2, NR, 2)),
         ],
         compiler_params=pltpu.CompilerParams(
-            collective_id=1, has_side_effects=True, vmem_limit_bytes=28 * MIB
+            collective_id=1, has_side_effects=True, vmem_limit_bytes=34 * MIB
         ),
         name="panel_factors",
     )(b, s, t, core)
@@ -650,7 +666,7 @@
         in_specs=[vmem, vmem, vmem],
         out_specs=hbm,
         scratch_shapes=[pltpu.VMEM((n, UR, COLS), jnp.bfloat16), pltpu.SemaphoreType.DMA((n,))],
-        compiler_params=pltpu.CompilerParams(vmem_limit_bytes=10 * MIB),
+        compiler_params=pltpu.CompilerParams(vmem_limit_bytes=12 * MIB),
         name="panel_update",
     )(left, right, grid)
 

time: 213 us -> 204 us (0.958)
  Pallas kernels: 206 us -> 195 us
    pallas_call x1, Pallas kernels: 72.2 us -> 63 us  [factors(): pl.pallas_call(factor_kernel, out_shape=(jax.ShapeDtypeStruct((ROWS, RANK...]
where the time goes in v3:
time: 204 us; the launch traced here: 202 us
  Pallas kernels  195 us (96%)
  local copies, waits for them, and re-layouts  3.41 us (2%)
  other arithmetic  2.4 us (1%)
    pallas_call x1, Pallas kernels, exchange(): pl.pallas_call(exchange_kernel, out_shape=(jax.ShapeDtypeStruct((ND, CAP,...  115 us
    pallas_call x1, Pallas kernels, factors(): pl.pallas_call(factor_kernel, out_shape=(jax.ShapeDtypeStruct((ROWS, RANK...  63 us
    pallas_call x1, Pallas kernels, assemble(): pl.pallas_call(assemble_kernel, out_shape=(jax.ShapeDtypeStruct((ROWS, CO...  8.41 us
    pallas_call x1, Pallas kernels, update(): pl.pallas_call(update_kernel, out_shape=jax.ShapeDtypeStruct((ROWS, COLS)...  8.09 us

profile of v3, /device:TPU:80, one launch (start us, length us, event | category | flops | bytes accessed | tf_op | source)
XLA Modules:
  0.0 201.6 jit_solution(10970362582312110528)
XLA Ops:
  0.7 0.9 convert_reduce_fusion
  1.6 0.7 broadcast_add_fusion.1
  2.2 0.7 iota_compare_fusion.1
  2.9 0.2 select_reduce_fusion
  3.1 0.1 copy.11
  3.2 0.0 copy-start
  3.3 0.0 copy-start.1
  3.3 2.3 %copy-done.1 = bf16[128,128,128]{2,1,0:T(8,128)(2,1)S(1)} copy-done((bf16[128,128,128]{2,1,0:T(8,128)(2,1)S(1)}, bf16[128,128,128]{2,1,0:T(8,128)(2,1)}, u32[]{:S(2)}) %copy-start.1) | copy-done | bytes 4194328
  5.6 0.0 copy-start.2
  5.6 115.4 %tile_exchange.1 = (bf16[128,2,128,128]{3,2,1,0:T(8,128)(2,1)S(1)}, s32[128,1,128]{2,1,0:T(1,128)S(1)}) custom-call(s32[2,128]{1,0:T(2,128)S(1)} %get-tuple-element.22.idx_ref, s32[128,1,128]{2,1,0:T(1,128)S(1)} %pad.4.slot_ref, bf16[128,128,128]{2,1,0:T(8,128)(2,1)S(1)} %copy-done.1), custom_call_target="tpu_custom_call" | custom-call | tf_op jit(solution)/shard_map/tile_exchange/pallas_call | solution.py:109
  121.0 0.0 copy-done
  121.0 0.0 copy-done.2
  121.0 0.0 copy-start.3
  121.0 0.9 copy-done.3
  121.9 0.0 copy-start.4
  121.9 8.4 %extend_add.1 = (f32[1024,2048]{1,0:T(8,128)S(1)}, bf16[1024,512]{1,0:T(8,128)(2,1)S(1)}, bf16[256,2048]{1,0:T(8,128)(2,1)S(1)}, bf16[256,512]{1,0:T(8,128)(2,1)S(1)}) custom-call(s32[128,128]{1,0:T(8,128)S(1)} %bitcast.7, bf16[1024,2048]{1,0:T(8,128)(2,1)S(1)} %copy-done, bf16[128,2,128,128]{3,2,1,0:T(8,128)(2,1)S(1)} %get-tuple-element.14.got_ref, ...), custom_call_target="tpu_custom_call" | custom-call | tf_op jit(solution)/shard_map/extend_add/pallas_call | solution.py:194
  130.3 0.0 copy-done.4
  130.3 63.0 %panel_factors.1 = (bf16[1024,1280]{1,0:T(8,128)(2,1)S(1)}, bf16[4,1280,512]{2,1,0:T(8,128)(2,1)S(1)}) custom-call(bf16[1024,512]{1,0:T(8,128)(2,1)S(1)} %get-tuple-element.15.b_ref, bf16[256,2048]{1,0:T(8,128)(2,1)S(1)} %get-tuple-element.16.s_ref, bf16[256,512]{1,0:T(8,128)(2,1)S(1)} %get-tuple-element.17.t_ref, bf16[128,128]{1,0:T(8,128)(2,1)S(1)} %copy-done.4), custom_call_target="tpu_custom_call" | custom-call | tf_op jit(solution)/shard_map/panel_factors/pallas_call | solution.py:603
  193.4 8.1 %panel_update.1 = bf16[1024,2048]{1,0:T(8,128)(2,1)} custom-call(bf16[1024,1280]{1,0:T(8,128)(2,1)S(1)} %get-tuple-element.18.left, bf16[4,1280,512]{2,1,0:T(8,128)(2,1)S(1)} %get-tuple-element.19.right, f32[1024,2048]{1,0:T(8,128)S(1)} %get-tuple-element.20.grid), custom_call_target="tpu_custom_call" | custom-call | tf_op jit(solution)/shard_map/panel_update/pallas_call | solution.py:663
  (4 shorter events, 0.1 us)
Async XLA Ops:
  3.2 117.8 %copy-start = (bf16[1024,2048]{1,0:T(8,128)(2,1)S(1)}, bf16[1024,2048]{1,0:T(8,128)(2,1)}, u32[]{:S(2)}) copy-start(bf16[1024,2048]{1,0:T(8,128)(2,1)} %front_ref.1) | copy-start | bytes 12582916
  3.3 2.3 %copy-start.1 = (bf16[128,128,128]{2,1,0:T(8,128)(2,1)S(1)}, bf16[128,128,128]{2,1,0:T(8,128)(2,1)}, u32[]{:S(2)}) copy-start(bf16[128,128,128]{2,1,0:T(8,128)(2,1)} %tiles_ref.1) | copy-start | bytes 12582916
  5.6 115.4 %copy-start.2 = (bf16[512,128]{1,0:T(8,128)(2,1)S(1)}, bf16[512,128]{1,0:T(8,128)(2,1)}, u32[]{:S(2)}) copy-start(bf16[512,128]{1,0:T(8,128)(2,1)} %omega_ref.1) | copy-start | bytes 393220
  121.0 0.9 copy-start.3
  121.9 8.4 %copy-start.4 = (bf16[128,128]{1,0:T(8,128)(2,1)S(1)}, bf16[128,128]{1,0:T(8,128)(2,1)}, u32[]{:S(2)}) copy-start(bf16[128,128]{1,0:T(8,128)(2,1)} %core_ref.1) | copy-start | bytes 98308

commit v4 on v3

--- a/solution.py
+++ b/solution.py
@@ -129,9 +129,15 @@
     )(idx, slots, tiles)
 
 
-def assemble_kernel(slot_ref, front_ref, got_ref, omega_ref, psi_ref, grid, b_ref, s_ref, t_ref):
+def assemble_kernel(
+    gslot_ref, front_ref, got_ref, omega_ref, psi_ref, grid, b_ref, s_ref, t_ref, turned, slot_ref, sem
+):
     r = lax.axis_index("row")
     c = lax.axis_index("col")
+
+    turned[...] = gslot_ref[...].T[:8]
+    to_scalar = pltpu.make_async_copy(turned, slot_ref, sem)
+    to_scalar.start()
 
     def widen(i, carry):
         rows = pl.ds(pl.multiple_of(i * 64, 64), 64)
@@ -140,32 +146,36 @@
 
     lax.fori_loop(0, ROWS // 64, widen, 0)
 
+    to_scalar.wait()
+
+    def add_at(slot, source, k):
+        rows = pl.ds(pl.multiple_of(div(slot, COLS // TILE) * TILE, TILE), TILE)
+        cols = pl.ds(pl.multiple_of(rem(slot, COLS // TILE) * TILE, TILE), TILE)
+        grid[rows, cols] += got_ref[source, k].astype(jnp.float32)
+
     def add(source, carry):
-        for k in range(CAP):
-            slot = slot_ref[source, k]
-
-            @pl.when(slot >= 0)
-            def _():
-                rows = pl.ds(pl.multiple_of(div(slot, COLS // TILE) * TILE, TILE), TILE)
-                cols = pl.ds(pl.multiple_of(rem(slot, COLS // TILE) * TILE, TILE), TILE)
-                grid[rows, cols] += got_ref[source, k].astype(jnp.float32)
+        slot = slot_ref[0, source]
+
+        @pl.when(slot >= 0)
+        def _():
+            add_at(slot, source, 0)
+            second = slot_ref[1, source]
+
+            @pl.when(second >= 0)
+            def _():
+                add_at(second, source, 1)
 
         return carry
 
-    lax.fori_loop(0, ND, add, 0)
+    lax.fori_loop(0, ND, add, 0, unroll=4)
 
     @pl.when(c < CSRC)
     def _():
-        def rows_of(i, carry):
-            rows = pl.ds(pl.multiple_of(i * 256, 256), 256)
-            for k in range(4):
-                block = grid[rows, k * PB : (k + 1) * PB].astype(jnp.bfloat16)
-                b_ref[rows, k * SK : (k + 1) * SK] = jnp.dot(
-                    block, omega_ref[...], preferred_element_type=jnp.float32
-                ).astype(jnp.bfloat16)
-            return carry
-
-        lax.fori_loop(0, ROWS // 256, rows_of, 0)
+        for k in range(4):
+            block = grid[:, k * PB : (k + 1) * PB].astype(jnp.bfloat16)
+            b_ref[:, k * SK : (k + 1) * SK] = jnp.dot(
+                block, omega_ref[...], preferred_element_type=jnp.float32
+            ).astype(jnp.bfloat16)
 
     @pl.when(r < RSRC)
     def _():
@@ -199,8 +209,13 @@
             jax.ShapeDtypeStruct((2 * SK, COLS), jnp.bfloat16),
             jax.ShapeDtypeStruct((2 * SK, 4 * SK), jnp.bfloat16),
         ),
-        in_specs=[pl.BlockSpec(memory_space=pltpu.SMEM), vmem, vmem, vmem, vmem],
+        in_specs=[vmem] * 5,
         out_specs=(vmem, vmem, vmem, vmem),
+        scratch_shapes=[
+            pltpu.VMEM((8, TILE), jnp.int32),
+            pltpu.SMEM((8, TILE), jnp.int32),
+            pltpu.SemaphoreType.DMA,
+        ],
         compiler_params=pltpu.CompilerParams(vmem_limit_bytes=6 * MIB),
         name="extend_add",
     )(slots, front, got, omega, psi)
@@ -515,33 +530,6 @@
     core = core_ref[...]
     eliminate(tall, core, state, lmat, rmat, {1: lambda: relay_both(1), 5: lambda: relay_both(2)})
 
-    def right_block(i, carry):
-        xx = rem(x + i, 4)
-        for zz in range(4):
-            piece = xx * 4 + zz
-            dz = rem(zz - z + 4, 4)
-
-            @pl.when(dz != 0)
-            def _():
-                settle(0, piece, dz)
-
-            @pl.when(i != 0)
-            def _():
-                settle(1, piece, i)
-
-        block = jnp.concatenate([sall[xx * 4 + h].reshape(RANK, TILE) for h in range(4)], axis=1)
-        panel = c * (COLS // PB) + xx
-        for q in range(RSRC):
-            lo, hi = q * 2 * SK, (q + 1) * 2 * SK
-            out = jnp.dot(rmat[lo:hi, :hi], block[:hi], preferred_element_type=f32)
-            for j in range(2):
-                part = out[j * SK : (j + 1) * SK]
-                part = jnp.where(2 * q + j < panel, part, jnp.zeros_like(part))
-                right[xx, lo + j * SK : lo + (j + 1) * SK, :] = part.astype(bf16)
-        return carry
-
-    lax.fori_loop(0, BLOCKS, right_block, 0)
-
     wait_other(b3)
 
     def left_rows(i, carry):
@@ -557,6 +545,34 @@
         return carry
 
     lax.fori_loop(0, ROWS // PB, left_rows, 0)
+
+    def right_block(i, carry):
+        dx = i + div(i, 2) - 2 * div(i, 3)
+        xx = rem(x + dx, 4)
+        for zz in range(4):
+            piece = xx * 4 + zz
+            dz = rem(zz - z + 4, 4)
+
+            @pl.when(dz != 0)
+            def _():
+                settle(0, piece, dz)
+
+            @pl.when(dx != 0)
+            def _():
+                settle(1, piece, dx)
+
+        block = jnp.concatenate([sall[xx * 4 + h].reshape(RANK, TILE) for h in range(4)], axis=1)
+        panel = c * (COLS // PB) + xx
+        for q in range(RSRC):
+            lo, hi = q * 2 * SK, (q + 1) * 2 * SK
+            out = jnp.dot(rmat[lo:hi, :hi], block[:hi], preferred_element_type=f32)
+            for j in range(2):
+                part = out[j * SK : (j + 1) * SK]
+                part = jnp.where(2 * q + j < panel, part, jnp.zeros_like(part))
+                right[xx, lo + j * SK : lo + (j + 1) * SK, :] = part.astype(bf16)
+        return carry
+
+    lax.fori_loop(0, BLOCKS, right_block, 0)
 
     @pl.when(r < RSRC)
     def _():
@@ -637,23 +653,25 @@
     def of_rows(i):
         return pl.ds(pl.multiple_of(i * UR, UR), UR)
 
-    def store(i):
-        return pltpu.make_async_copy(obuf.at[i], out_ref.at[of_rows(i)], osem.at[i])
+    def store(i, q):
+        cols = pl.ds(pl.multiple_of(q * WIDE, WIDE), WIDE)
+        return pltpu.make_async_copy(obuf.at[i, :, cols], out_ref.at[of_rows(i), cols], osem.at[i, q])
 
     def rows(i, carry):
         def block(q, carry):
             cols = pl.ds(pl.multiple_of(q * WIDE, WIDE), WIDE)
             product = jnp.dot(left[of_rows(i), :], right[q], preferred_element_type=f32)
             obuf[i, :, cols] = (grid[of_rows(i), cols] - product).astype(jnp.bfloat16)
+            store(i, q).start()
             return carry
 
         lax.fori_loop(0, BLOCKS, block, 0)
-        store(i).start()
         return carry
 
     lax.fori_loop(0, n, rows, 0)
     for i in range(n):
-        store(i).wait()
+        for q in range(BLOCKS):
+            store(i, q).wait()
 
 
 def update(left, right, grid):
@@ -665,7 +683,7 @@
         out_shape=jax.ShapeDtypeStruct((ROWS, COLS), jnp.bfloat16),
         in_specs=[vmem, vmem, vmem],
         out_specs=hbm,
-        scratch_shapes=[pltpu.VMEM((n, UR, COLS), jnp.bfloat16), pltpu.SemaphoreType.DMA((n,))],
+        scratch_shapes=[pltpu.VMEM((n, UR, COLS), jnp.bfloat16), pltpu.SemaphoreType.DMA((n, BLOCKS))],
         compiler_params=pltpu.CompilerParams(vmem_limit_bytes=12 * MIB),
         name="panel_update",
     )(left, right, grid)

time: 204 us -> 200 us (0.980)
  Pallas kernels: 195 us -> 191 us
    pallas_call x1, Pallas kernels: 8.41 us -> 5.15 us  [assemble(): pl.pallas_call(assemble_kernel, out_shape=(jax.ShapeDtypeStruct((ROWS, CO...]
where the time goes in v4:
time: 200 us; the launch traced here: 197 us
  Pallas kernels  191 us (96%)
  local copies, waits for them, and re-layouts  3.41 us (2%)
  other arithmetic  2.4 us (1%)
    pallas_call x1, Pallas kernels, exchange(): pl.pallas_call(exchange_kernel, out_shape=(jax.ShapeDtypeStruct((ND, CAP,...  115 us
    pallas_call x1, Pallas kernels, factors(): pl.pallas_call(factor_kernel, out_shape=(jax.ShapeDtypeStruct((ROWS, RANK...  62.6 us
    pallas_call x1, Pallas kernels, update(): pl.pallas_call(update_kernel, out_shape=jax.ShapeDtypeStruct((ROWS, COLS)...  7.62 us
    pallas_call x1, Pallas kernels, assemble(): pl.pallas_call(assemble_kernel, out_shape=(jax.ShapeDtypeStruct((ROWS, CO...  5.15 us

profile of v4, /device:TPU:80, one launch (start us, length us, event | category | flops | bytes accessed | tf_op | source)
XLA Modules:
  0.0 197.5 jit_solution(14615284247302173787)
XLA Ops:
  0.7 0.9 convert_reduce_fusion
  1.6 0.7 broadcast_add_fusion.1
  2.2 0.7 iota_compare_fusion.1
  2.9 0.2 select_reduce_fusion
  3.1 0.1 copy.11
  3.2 0.0 copy-start
  3.3 0.0 copy-start.1
  3.3 2.3 %copy-done.1 = bf16[128,128,128]{2,1,0:T(8,128)(2,1)S(1)} copy-done((bf16[128,128,128]{2,1,0:T(8,128)(2,1)S(1)}, bf16[128,128,128]{2,1,0:T(8,128)(2,1)}, u32[]{:S(2)}) %copy-start.1) | copy-done | bytes 4194328
  5.6 0.0 copy-start.2
  5.6 115.4 %tile_exchange.1 = (bf16[128,2,128,128]{3,2,1,0:T(8,128)(2,1)S(1)}, s32[128,1,128]{2,1,0:T(1,128)S(1)}) custom-call(s32[2,128]{1,0:T(2,128)S(1)} %get-tuple-element.22.idx_ref, s32[128,1,128]{2,1,0:T(1,128)S(1)} %pad.4.slot_ref, bf16[128,128,128]{2,1,0:T(8,128)(2,1)S(1)} %copy-done.1), custom_call_target="tpu_custom_call" | custom-call | tf_op jit(solution)/shard_map/tile_exchange/pallas_call | solution.py:109
  121.0 0.0 copy-done
  121.0 0.0 copy-done.2
  121.0 0.0 copy-start.3
  121.0 0.9 copy-done.3
  121.9 0.0 copy-start.4
  121.9 5.2 %extend_add.1 = (f32[1024,2048]{1,0:T(8,128)S(1)}, bf16[1024,512]{1,0:T(8,128)(2,1)S(1)}, bf16[256,2048]{1,0:T(8,128)(2,1)S(1)}, bf16[256,512]{1,0:T(8,128)(2,1)S(1)}) custom-call(s32[128,128]{1,0:T(8,128)S(1)} %bitcast.7, bf16[1024,2048]{1,0:T(8,128)(2,1)S(1)} %copy-done, bf16[128,2,128,128]{3,2,1,0:T(8,128)(2,1)S(1)} %get-tuple-element.14.got_ref, ...), custom_call_target="tpu_custom_call" | custom-call | tf_op jit(solution)/shard_map/extend_add/pallas_call | solution.py:204
  127.1 0.0 copy-done.4
  127.1 62.6 %panel_factors.1 = (bf16[1024,1280]{1,0:T(8,128)(2,1)S(1)}, bf16[4,1280,512]{2,1,0:T(8,128)(2,1)S(1)}) custom-call(bf16[1024,512]{1,0:T(8,128)(2,1)S(1)} %get-tuple-element.15.b_ref, bf16[256,2048]{1,0:T(8,128)(2,1)S(1)} %get-tuple-element.16.s_ref, bf16[256,512]{1,0:T(8,128)(2,1)S(1)} %get-tuple-element.17.t_ref, bf16[128,128]{1,0:T(8,128)(2,1)S(1)} %copy-done.4), custom_call_target="tpu_custom_call" | custom-call | tf_op jit(solution)/shard_map/panel_factors/pallas_call | solution.py:619
  189.7 7.6 %panel_update.1 = bf16[1024,2048]{1,0:T(8,128)(2,1)} custom-call(bf16[1024,1280]{1,0:T(8,128)(2,1)S(1)} %get-tuple-element.18.left, bf16[4,1280,512]{2,1,0:T(8,128)(2,1)S(1)} %get-tuple-element.19.right, f32[1024,2048]{1,0:T(8,128)S(1)} %get-tuple-element.20.grid), custom_call_target="tpu_custom_call" | custom-call | tf_op jit(solution)/shard_map/panel_update/pallas_call | solution.py:681
  (4 shorter events, 0.1 us)
Async XLA Ops:
  3.2 117.8 %copy-start = (bf16[1024,2048]{1,0:T(8,128)(2,1)S(1)}, bf16[1024,2048]{1,0:T(8,128)(2,1)}, u32[]{:S(2)}) copy-start(bf16[1024,2048]{1,0:T(8,128)(2,1)} %front_ref.1) | copy-start | bytes 12582916
  3.3 2.3 %copy-start.1 = (bf16[128,128,128]{2,1,0:T(8,128)(2,1)S(1)}, bf16[128,128,128]{2,1,0:T(8,128)(2,1)}, u32[]{:S(2)}) copy-start(bf16[128,128,128]{2,1,0:T(8,128)(2,1)} %tiles_ref.1) | copy-start | bytes 12582916
  5.6 115.4 %copy-start.2 = (bf16[512,128]{1,0:T(8,128)(2,1)S(1)}, bf16[512,128]{1,0:T(8,128)(2,1)}, u32[]{:S(2)}) copy-start(bf16[512,128]{1,0:T(8,128)(2,1)} %omega_ref.1) | copy-start | bytes 393220
  121.0 0.9 copy-start.3
  121.9 5.2 %copy-start.4 = (bf16[128,128]{1,0:T(8,128)(2,1)S(1)}, bf16[128,128]{1,0:T(8,128)(2,1)}, u32[]{:S(2)}) copy-start(bf16[128,128]{1,0:T(8,128)(2,1)} %core_ref.1) | copy-start | bytes 98308

commit v5 on v4

--- a/solution.py
+++ b/solution.py
@@ -521,14 +521,16 @@
     for half in range(2):
         relay_second(half, STEPS[0], 1)
     post_far(t3)
-    wait_other(t3)
 
     def relay_both(m):
         for half in range(2):
             relay_second(half, STEPS[m], 1 + m)
 
+    relay_both(1)
+    wait_other(t3)
+
     core = core_ref[...]
-    eliminate(tall, core, state, lmat, rmat, {1: lambda: relay_both(1), 5: lambda: relay_both(2)})
+    eliminate(tall, core, state, lmat, rmat, {2: lambda: relay_both(2)})
 
     wait_other(b3)
 
@@ -699,7 +701,7 @@
     named = strip[None, :, None] == owners[None, None, :]
     hit = named & (ranks[None, None, :] == jnp.arange(CAP, dtype=jnp.int32)[:, None, None])
     idx = jnp.sum(jnp.where(hit, strip[None, None, :], 0), axis=2)
-    slots = jnp.sum(jnp.where(hit & valid[None, None, :], dest_slot[None, None, :] + 1, 0), axis=2) - 1
+    slots = jnp.max(jnp.where(hit & valid[None, None, :], dest_slot[None, None, :], -1), axis=2)
     slots = jnp.pad(slots.T[:, None, :], ((0, 0), (0, 0), (0, TILE - CAP)))
     got, got_slots = exchange(idx, slots, tiles)
     grid, b, s, t = assemble(got_slots[:, 0, :], front, got, omega, psi)

time: 200 us -> 201 us (level); the launches traced: 197 us -> 201 us
  Pallas kernels: 191 us -> 195 us
    pallas_call x1, Pallas kernels: 62.6 us -> 66.2 us  [factors(): pl.pallas_call(factor_kernel, out_shape=(jax.ShapeDtypeStruct((ROWS, RANK...]
where the time goes in v5:
time: 201 us
  Pallas kernels  195 us (97%)
  local copies, waits for them, and re-layouts  3.41 us (2%)
  other arithmetic  2.39 us (1%)
    pallas_call x1, Pallas kernels, exchange(): pl.pallas_call(exchange_kernel, out_shape=(jax.ShapeDtypeStruct((ND, CAP,...  115 us
    pallas_call x1, Pallas kernels, factors(): pl.pallas_call(factor_kernel, out_shape=(jax.ShapeDtypeStruct((ROWS, RANK...  66.2 us
    pallas_call x1, Pallas kernels, update(): pl.pallas_call(update_kernel, out_shape=jax.ShapeDtypeStruct((ROWS, COLS)...  7.62 us
    pallas_call x1, Pallas kernels, assemble(): pl.pallas_call(assemble_kernel, out_shape=(jax.ShapeDtypeStruct((ROWS, CO...  5.31 us

profile of v5, /device:TPU:80, one launch (start us, length us, event | category | flops | bytes accessed | tf_op | source)
XLA Modules:
  0.0 201.2 jit_solution(10041780675806251391)
XLA Ops:
  0.7 0.9 convert_reduce_fusion
  1.6 0.7 iota_compare_fusion.1
  2.3 0.8 select_reduce_fusion
  3.1 0.1 copy.9
  3.2 0.0 copy-start
  3.2 0.0 copy-start.1
  3.3 2.3 %copy-done.1 = bf16[128,128,128]{2,1,0:T(8,128)(2,1)S(1)} copy-done((bf16[128,128,128]{2,1,0:T(8,128)(2,1)S(1)}, bf16[128,128,128]{2,1,0:T(8,128)(2,1)}, u32[]{:S(2)}) %copy-start.1) | copy-done | bytes 4194328
  5.6 0.0 copy-start.2
  5.6 115.4 %tile_exchange.1 = (bf16[128,2,128,128]{3,2,1,0:T(8,128)(2,1)S(1)}, s32[128,1,128]{2,1,0:T(1,128)S(1)}) custom-call(s32[2,128]{1,0:T(2,128)S(1)} %get-tuple-element.22.idx_ref, s32[128,1,128]{2,1,0:T(1,128)S(1)} %pad.4.slot_ref, bf16[128,128,128]{2,1,0:T(8,128)(2,1)S(1)} %copy-done.1), custom_call_target="tpu_custom_call" | custom-call | tf_op jit(solution)/shard_map/tile_exchange/pallas_call | solution.py:109
  121.0 0.0 copy-done
  121.0 0.0 copy-done.2
  121.0 0.0 copy-start.3
  121.0 0.9 copy-done.3
  121.9 0.0 copy-start.4
  121.9 5.3 %extend_add.1 = (f32[1024,2048]{1,0:T(8,128)S(1)}, bf16[1024,512]{1,0:T(8,128)(2,1)S(1)}, bf16[256,2048]{1,0:T(8,128)(2,1)S(1)}, bf16[256,512]{1,0:T(8,128)(2,1)S(1)}) custom-call(s32[128,128]{1,0:T(8,128)S(1)} %bitcast.7, bf16[1024,2048]{1,0:T(8,128)(2,1)S(1)} %copy-done, bf16[128,2,128,128]{3,2,1,0:T(8,128)(2,1)S(1)} %get-tuple-element.14.got_ref, ...), custom_call_target="tpu_custom_call" | custom-call | tf_op jit(solution)/shard_map/extend_add/pallas_call | solution.py:204
  127.2 0.0 copy-done.4
  127.2 66.2 %panel_factors.1 = (bf16[1024,1280]{1,0:T(8,128)(2,1)S(1)}, bf16[4,1280,512]{2,1,0:T(8,128)(2,1)S(1)}) custom-call(bf16[1024,512]{1,0:T(8,128)(2,1)S(1)} %get-tuple-element.15.b_ref, bf16[256,2048]{1,0:T(8,128)(2,1)S(1)} %get-tuple-element.16.s_ref, bf16[256,512]{1,0:T(8,128)(2,1)S(1)} %get-tuple-element.17.t_ref, bf16[128,128]{1,0:T(8,128)(2,1)S(1)} %copy-done.4), custom_call_target="tpu_custom_call" | custom-call | tf_op jit(solution)/shard_map/panel_factors/pallas_call | solution.py:621
  193.4 7.6 %panel_update.1 = bf16[1024,2048]{1,0:T(8,128)(2,1)} custom-call(bf16[1024,1280]{1,0:T(8,128)(2,1)S(1)} %get-tuple-element.18.left, bf16[4,1280,512]{2,1,0:T(8,128)(2,1)S(1)} %get-tuple-element.19.right, f32[1024,2048]{1,0:T(8,128)S(1)} %get-tuple-element.20.grid), custom_call_target="tpu_custom_call" | custom-call | tf_op jit(solution)/shard_map/panel_update/pallas_call | solution.py:683
  (3 shorter events, 0.1 us)
Async XLA Ops:
  3.2 117.8 %copy-start = (bf16[1024,2048]{1,0:T(8,128)(2,1)S(1)}, bf16[1024,2048]{1,0:T(8,128)(2,1)}, u32[]{:S(2)}) copy-start(bf16[1024,2048]{1,0:T(8,128)(2,1)} %front_ref.1) | copy-start | bytes 12582916
  3.2 2.3 %copy-start.1 = (bf16[128,128,128]{2,1,0:T(8,128)(2,1)S(1)}, bf16[128,128,128]{2,1,0:T(8,128)(2,1)}, u32[]{:S(2)}) copy-start(bf16[128,128,128]{2,1,0:T(8,128)(2,1)} %tiles_ref.1) | copy-start | bytes 12582916
  5.6 115.4 %copy-start.2 = (bf16[512,128]{1,0:T(8,128)(2,1)S(1)}, bf16[512,128]{1,0:T(8,128)(2,1)}, u32[]{:S(2)}) copy-start(bf16[512,128]{1,0:T(8,128)(2,1)} %omega_ref.1) | copy-start | bytes 393220
  121.0 0.9 copy-start.3
  121.9 5.3 %copy-start.4 = (bf16[128,128]{1,0:T(8,128)(2,1)S(1)}, bf16[128,128]{1,0:T(8,128)(2,1)}, u32[]{:S(2)}) copy-start(bf16[128,128]{1,0:T(8,128)(2,1)} %core_ref.1) | copy-start | bytes 98308
